TPU v7x, 256 devices: a whole 4x4x8 slice. The times are simulated.
256 devices in a mesh: sector: 8 (over x, core), slab: 32 (over y, z).
Axes of the slice: x: 4, y: 4, z: 8, core: 2. Of those that a mesh axis runs over, the one named last changes fastest.
Arguments:
- pressure: float32 [128, 512, 128], P('slab', 'sector'), may hold values from -6 to 6
- saturation: float32 [2, 128, 512, 128], P(None, 'slab', 'sector'), may hold values from 0.05 to 0.45
- old_mass: float32 [3, 128, 512, 128], P(None, 'slab', 'sector'), may hold values from 0 to 2.4
- pore_volume: float32 [128, 512, 128], P('slab', 'sector'), may hold values from 0.5 to 2
- transmissibility: float32 [3, 128, 512, 128], P(None, 'slab', 'sector'), may hold values from 0.2 to 5
- upwind_bits: int32 [128, 512, 128], P('slab', 'sector'), may hold values from 0 to 511
- fault_cell: int32 [32, 8, 8, 1024], P('slab', 'sector'), may hold values from 0 to 32767
- fault_count: int32 [32, 8, 8], P('slab', 'sector'), may hold values from 0 to 1024, as said below
- fault_trans: float32 [32, 8, 8, 1024], P('slab', 'sector'), as said below
- fault_upwind: int32 [32, 8, 8, 1024], P('slab', 'sector'), may hold values from 0 to 7, as said below
Outputs:
- residual: float32 [3, 128, 512, 128], P(None, 'slab', 'sector')
- pressure_update: float32 [128, 512, 128], P('slab', 'sector')
Inputs may be any that keep to these rules, and one draw needn't show every extreme that they name: `fault_count`: symmetric in its two sector dimensions, zero where they are equal; for every slab index some pair of sectors has exactly 1024 live slots. `fault_trans`: entry [t, s, e, j] equals entry [t, e, s, j]. `fault_upwind`: for s different from e, entries [t, s, e, j] and [t, e, s, j] add up to 7.
All inputs are finite; a program needn't handle non-finite values.
Results may differ from a plain program's by a relative error of at most 0.0003.
Values sent between devices are 32-bit elements; how exact they have to be, the bound alone decides.
A program may use at most 128 MiB of HBM per device.

v0:
```python
import jax
import jax.numpy as jnp
from jax import lax
from jax.sharding import PartitionSpec as P

SWEEPS = 4


COMPRESS = (0.0002, 0.0005, 0.002)
VISCOSITY = (1.0, 3.0, 0.5)
RELAXATION = 2.0 / 3.0


def padded_2(cells, sides, width):
    for axis, dim in sides:
        count = lax.axis_size(axis)
        ends = count - 1
        head = lax.slice_in_dim(cells, 0, width, axis=dim)
        tail = lax.slice_in_dim(cells, cells.shape[dim] - width, cells.shape[dim], axis=dim)
        cells = jnp.concatenate(
            [
                lax.ppermute(tail, axis, [(i, (i + 1) % count) for i in range(ends)]),
                cells,
                lax.ppermute(head, axis, [((i + 1) % count, i) for i in range(ends)]),
            ],
            axis=dim,
        )
    return cells


def phase_state(saturation):
    water = saturation[0]
    gas_part = saturation[1]
    saturations = jnp.stack([water, 1.0 - water - gas_part, gas_part])
    mobility = jnp.stack(
        [saturations[phase] * saturations[phase] / VISCOSITY[phase] for phase in range(3)]
    )
    return (saturations, mobility)


def accumulation(pressure, saturations, pore_volume, old_mass):
    masses = jnp.stack(
        [
            pore_volume * saturations[phase] * (1.0 + COMPRESS[phase] * pressure)
            for phase in range(3)
        ]
    )
    storage = pore_volume * (
        saturations[0] * COMPRESS[0] + saturations[1] * COMPRESS[1] + saturations[2] * COMPRESS[2]
    )
    return (masses - old_mass, storage)


def upwind_flags(words, first_bit):
    return jnp.stack(
        [jnp.bitwise_and(jnp.right_shift(words, first_bit + phase), 1) for phase in range(3)]
    )


def face_terms(
    low_pressure,
    low_mobility,
    low_trans,
    low_words,
    high_pressure,
    high_mobility,
    face_valid,
    direction,
):
    flags = upwind_flags(low_words, 3 * direction)
    upstream = jnp.where(flags == 1, low_mobility, high_mobility)
    weight = low_trans * face_valid
    face_flux = weight * upstream * (low_pressure - high_pressure)
    coupling = weight * (upstream[0] + upstream[1] + upstream[2])
    return (face_flux, coupling)


def fault_terms(own_pressure, own_mobility, far_pressure, far_mobility, weight, words):
    flags = upwind_flags(words, 0)
    upstream = jnp.where(flags == 1, own_mobility, far_mobility)
    face_flux = weight * upstream * (own_pressure - far_pressure)
    coupling = weight * (upstream[0] + upstream[1] + upstream[2])
    return (face_flux, coupling)


def coarse_solve(coarse_rows):
    store = coarse_rows[0]
    link = coarse_rows[1]
    source = coarse_rows[2]
    zero = jnp.zeros((1,), jnp.float32)
    below = jnp.concatenate([zero, link[:-1]])
    diagonal = store + link + below
    upper = jnp.concatenate([-link[:-1], zero])
    return lax.linalg.tridiagonal_solve(-below, diagonal, upper, source[:, None])[:, 0]


def body(
    pressure,
    saturation,
    old_mass,
    pore_volume,
    transmissibility,
    upwind_bits,
    fault_cell,
    fault_count,
    fault_trans,
    fault_upwind,
):
    layer_count, row_count, column_count = pressure.shape
    sector_count = lax.axis_size("sector")
    slab_count = lax.axis_size("slab")
    slot_count = fault_cell.shape[3]
    layer_first = lax.axis_index("slab") * layer_count
    row_first = lax.axis_index("sector") * row_count
    total_layers = layer_count * slab_count
    total_rows = row_count * sector_count
    saturations, mobility = phase_state(saturation)
    residual, storage = accumulation(pressure, saturations, pore_volume, old_mass)
    face_layer = lax.broadcasted_iota(jnp.int32, (layer_count + 1, 1, 1), 0) + layer_first - 1
    valid_layer = ((face_layer >= 0) & (face_layer <= total_layers - 2)).astype(jnp.float32)
    face_row = lax.broadcasted_iota(jnp.int32, (1, row_count + 1, 1), 1) + row_first - 1
    valid_row = ((face_row >= 0) & (face_row <= total_rows - 2)).astype(jnp.float32)
    fields = jnp.concatenate([pressure[None], mobility], 0)
    stacked = jnp.concatenate(
        [fields, transmissibility[0:2], upwind_bits[None].astype(jnp.float32)], 0
    )
    extended = padded_2(stacked, (("slab", 1), ("sector", 2)), 1)
    words = extended[6].astype(jnp.int32)
    lower = extended[:, 0 : layer_count + 1, 1 : row_count + 1]
    higher = extended[:, 1 : layer_count + 2, 1 : row_count + 1]
    flux_layer, link_layer = face_terms(
        lower[0],
        lower[1:4],
        lower[4],
        words[0 : layer_count + 1, 1 : row_count + 1],
        higher[0],
        higher[1:4],
        valid_layer,
        0,
    )
    lower = extended[:, 1 : layer_count + 1, 0 : row_count + 1]
    higher = extended[:, 1 : layer_count + 1, 1 : row_count + 2]
    flux_row, link_row = face_terms(
        lower[0],
        lower[1:4],
        lower[5],
        words[1 : layer_count + 1, 0 : row_count + 1],
        higher[0],
        higher[1:4],
        valid_row,
        1,
    )
    column_flux, column_link = face_terms(
        pressure[..., :-1],
        mobility[..., :-1],
        transmissibility[2][..., :-1],
        upwind_bits[..., :-1],
        pressure[..., 1:],
        mobility[..., 1:],
        1.0,
        2,
    )
    flux_column = jnp.pad(column_flux, ((0, 0), (0, 0), (0, 0), (1, 1)))
    link_column = jnp.pad(column_link, ((0, 0), (0, 0), (1, 1)))
    residual = residual + (flux_layer[:, 1:] - flux_layer[:, :-1])
    residual = residual + (flux_row[:, :, 1:] - flux_row[:, :, :-1])
    residual = residual + (flux_column[..., 1:] - flux_column[..., :-1])
    diagonal = storage + (link_layer[1:] + link_layer[:-1])
    diagonal = diagonal + (link_row[:, 1:] + link_row[:, :-1])
    diagonal = diagonal + (link_column[..., 1:] + link_column[..., :-1])
    slot_cells = fault_cell.reshape(sector_count, slot_count)
    slot_live = (
        lax.broadcasted_iota(jnp.int32, (sector_count, slot_count), 1)
        < fault_count.reshape(sector_count, 1)
    ).astype(jnp.float32)
    flat_index = slot_cells.reshape(-1)
    own_fields = fields.reshape(4, -1)[:, flat_index].reshape(4, sector_count, slot_count)
    partner_fields = lax.all_to_all(own_fields, "sector", split_axis=1, concat_axis=1, tiled=True)
    fault_flux, fault_link = fault_terms(
        own_fields[0],
        own_fields[1:4],
        partner_fields[0],
        partner_fields[1:4],
        fault_trans.reshape(sector_count, slot_count) * slot_live,
        fault_upwind.reshape(sector_count, slot_count),
    )
    residual = (
        residual.reshape(3, -1)
        .at[:, flat_index]
        .add(fault_flux.reshape(3, -1))
        .reshape(3, layer_count, row_count, column_count)
    )
    diagonal = (
        diagonal.reshape(-1).at[flat_index].add(fault_link.reshape(-1)).reshape(pressure.shape)
    )
    fault_weight = fault_link.reshape(-1)
    pressure_rhs = -(residual[0] + residual[1] + residual[2])
    layer_rows = jnp.stack(
        [storage.sum(axis=(1, 2)), link_layer[1:].sum(axis=(1, 2)), pressure_rhs.sum(axis=(1, 2))]
    )
    summed = lax.psum(layer_rows, "sector")
    coarse_rows = lax.all_gather(summed, "slab", axis=1, tiled=True)
    coarse = coarse_solve(coarse_rows)
    update = jnp.broadcast_to(
        lax.dynamic_slice_in_dim(coarse, layer_first, layer_count)[:, None, None], pressure.shape
    )
    for sweep in range(SWEEPS):
        extended = padded_2(update, (("slab", 0), ("sector", 1)), 1)
        padded = jnp.pad(update, ((0, 0), (0, 0), (1, 1)))
        image = diagonal * update
        image = image - (
            link_layer[1:] * extended[2:, 1:-1] + link_layer[:-1] * extended[:-2, 1:-1]
        )
        image = image - (
            link_row[:, 1:] * extended[1:-1, 2:] + link_row[:, :-1] * extended[1:-1, :-2]
        )
        image = image - (
            link_column[..., 1:] * padded[..., 2:] + link_column[..., :-1] * padded[..., :-2]
        )
        own_update = update.reshape(-1)[flat_index].reshape(sector_count, slot_count)
        partner_update = lax.all_to_all(
            own_update, "sector", split_axis=0, concat_axis=0, tiled=True
        )
        extra = (
            jnp.zeros((layer_count * row_count * column_count,), jnp.float32)
            .at[flat_index]
            .add(fault_weight * partner_update.reshape(-1))
            .reshape(pressure.shape)
        )
        image = image - extra
        update = update + RELAXATION * (pressure_rhs - image) / diagonal
    return (residual, update)


def solution(mesh):
    placed = (
        P("slab", "sector", None),
        P(None, "slab", "sector", None),
        P(None, "slab", "sector", None),
        P("slab", "sector", None),
        P(None, "slab", "sector", None),
        P("slab", "sector", None),
        P("slab", "sector", None, None),
        P("slab", "sector", None),
        P("slab", "sector", None, None),
        P("slab", "sector", None, None),
    )
    return jax.shard_map(
        body,
        mesh=mesh,
        in_specs=placed,
        out_specs=(P(None, "slab", "sector", None), P("slab", "sector", None)),
        check_vma=False,
    )
```

profile of v0, /device:TPU:1, one launch (start us, length us, event | category | flops | bytes accessed | tf_op | source)
XLA Modules:
  0.0 1463.0 jit_solution(14116380467441960660)
XLA Ops:
  7.3 4.4 collective-permute-start
  15.2 8.4 copy.51
  23.7 33.5 %gather_fusion = f32[8192,4]{1,0:T(8,128)} fusion(f32[4,32768]{0,1:T(8,128)} %copy.51, s32[8192]{0:T(1024)S(1)} %broadcast_clamp_fusion), kind=kCustom, calls=%fused_computation | custom fusion | bytes 294912 | tf_op jit(solution)/shard_map/gather | solution.py:177
  60.6 5.3 all-to-all-start
  75.7 5.3 slice.2834
  98.3 8.7 copy.47
  107.0 51.4 %scatter_fusion = f32[3,32768]{0,1:T(8,128)} fusion(f32[3,32768]{0,1:T(8,128)} %bitcast.1532, s32[8192]{0:T(1024)S(1)} %bitcast.1549, f32[8192,3]{1,0:T(8,128)} %copy.55), kind=kCustom, calls=%fused_computation.5 | custom fusion | flops 24576 | bytes 327680 | tf_op jit(solution)/shard_map/scatter-add | solution.py:190
  158.3 26.9 %fusion = f32[32768]{0:T(1024)S(1)} fusion(f32[3,32768]{0,1:T(8,128)} %scatter_fusion), kind=kLoop, calls=%fused_computation.20 | loop fusion | flops 65536 | bytes 524288 | tf_op jit(solution)/shard_map/add | solution.py:197
  185.6 10.6 psum.7
  196.3 40.8 %all-gather = f32[32,4,3]{2,1,0:T(4,128)S(1)} all-gather(f32[1,4,3]{2,1,0:T(4,128)S(1)} %bitcast.1575), channel_id=1, replica_groups=mesh['sector'=8,'slab'=32] {'slab'}, dimensions={0}, use_global_device_ids=true | all-gather | bytes 1584 | tf_op jit(solution)/shard_map/all_gather | solution.py:202
  246.2 318.1 %while.32 = (s32[]{:T(128)}, f32[]{:T(128)}, f32[1]{0:T(128)}, f32[3,32]{1,0:T(4,128)S(1)}, f32[3,32,1]{1,2,0:T(1,128)S(1)}, /*index=5*/f32[3,32]{1,0:T(4,128)S(...) while((s32[]{:T(128)}, f32[]{:T(128)}, f32[1]{0:T(128)}, ...), condition=%wide.region_6.7_spmd, body=%wide.region_5.6_spmd.sunk | while | flops 194 | bytes 6297 | solution.py:94
  666.1 129.2 %while.33 = (s32[]{:T(128)}, f32[1]{0:T(128)}, f32[3,32,1]{1,2,0:T(1,128)S(1)}, f32[3,32,1]{1,2,0:T(1,128)S(1)}, f32[3,32]{1,0:T(4,128)S(1)}, /*index=5*/s32[]{:T(128)}, s32[]{:T(128)}) while((s32[]{:T(128)}, f32[1]{0:T(128)}, f32[3,32,1]{1,2,0:T(1,128)S(1)}, f32[3,32,1]{1,2,0:T(1,128)S(1)}, f32[3,32]{1,0:T(4,128)S(1)}, /*index=5*/s32[]{:T(128)}, ...), condition=%wide.region_8.9_spmd, body=%wide.region_7.8_spmd.sunk | while | flops 67 | bytes 3181 | solution.py:94
  837.1 4.0 collective-permute-start.5
  841.3 80.6 %gather_fusion.1 = f32[8192]{0:T(1024)} fusion(f32[32768]{0:T(1024)S(1)} %bitcast.1531, s32[8192]{0:T(1024)S(1)} %broadcast_clamp_fusion), kind=kCustom, calls=%fused_computation.1 | custom fusion | bytes 98304 | tf_op jit(solution)/shard_map/gather | solution.py:220
  921.8 18.6 %all-to-all-start.1 = ((f32[8,1,1024]{2,1,0:T(1,128)}), f32[8,1,1024]{2,1,0:T(1,128)S(1)}, u32[]{:S(2)}, u32[]{:S(2)}) async-start(f32[8,1,1024]{2,1,0:T(1,128)} %bitcast.697), calls=%async_computation.1 | async-start | bytes 65536 | tf_op jit(solution)/shard_map/all_to_all | solution.py:221
  946.1 44.3 %scatter_fusion.1 = f32[32768]{0:T(1024)S(1)} fusion(f32[32768]{0:T(1024)S(1)} %bitcast.1523, s32[8192]{0:T(1024)S(1)} %bitcast.1550, f32[8192]{0:T(1024)S(1)} %get-tuple-element.257), kind=kCustom, calls=%fused_computation.6 | custom fusion | flops 8192 | bytes 131072 | tf_op jit(solution)/shard_map/scatter-add | solution.py:194
  990.4 43.5 %scatter_custom_fusion.2 = f32[32768]{0:T(1024)S(1)} fusion(s32[8192]{0:T(1024)S(1)} %bitcast.1551, f32[8192]{0:T(1024)S(1)} %get-tuple-element.256, f32[]{:T(128)} %constant.128.clone.1), kind=kCustom, calls=%fused_computation.232 | custom fusion | flops 8192 | bytes 131076 | tf_op jit(solution)/shard_map/scatter-add | solution.py:227
  1037.9 80.6 %gather_fusion.2 = f32[8192]{0:T(1024)} fusion(f32[32768]{0:T(1024)S(1)} %bitcast.1529, s32[8192]{0:T(1024)S(1)} %broadcast_clamp_fusion), kind=kCustom, calls=%fused_computation.2 | custom fusion | bytes 98304 | tf_op jit(solution)/shard_map/gather | solution.py:220
  1118.4 4.6 all-to-all-start.2
  1125.0 3.6 collective-permute-start.11
  1128.6 43.2 %scatter_custom_fusion.3 = f32[32768]{0:T(1024)S(1)} fusion(s32[8192]{0:T(1024)S(1)} %bitcast.1552, f32[8192]{0:T(1024)S(1)} %mul.1266, f32[]{:T(128)} %constant.128.clone.1), kind=kCustom, calls=%fused_computation.230 | custom fusion | flops 8192 | bytes 131076 | tf_op jit(solution)/shard_map/scatter-add | solution.py:227
  1172.1 4.3 collective-permute-start.13
  1177.7 80.6 %gather_fusion.3 = f32[8192]{0:T(1024)} fusion(f32[32768]{0:T(1024)S(1)} %bitcast.1530, s32[8192]{0:T(1024)S(1)} %broadcast_clamp_fusion), kind=kCustom, calls=%fused_computation.3 | custom fusion | bytes 98304 | tf_op jit(solution)/shard_map/gather | solution.py:220
  1258.3 4.6 all-to-all-start.3
  1264.8 3.6 collective-permute-start.15
  1268.5 43.2 %scatter_custom_fusion.4 = f32[32768]{0:T(1024)S(1)} fusion(s32[8192]{0:T(1024)S(1)} %bitcast.1553, f32[8192]{0:T(1024)S(1)} %mul.1275, f32[]{:T(128)} %constant.128.clone.1), kind=kCustom, calls=%fused_computation.228 | custom fusion | flops 8192 | bytes 131076 | tf_op jit(solution)/shard_map/scatter-add | solution.py:227
  1311.9 4.2 collective-permute-start.17
  1317.5 80.6 %gather_fusion.4 = f32[8192]{0:T(1024)} fusion(f32[32768]{0:T(1024)S(1)} %bitcast.1528, s32[8192]{0:T(1024)S(1)} %broadcast_clamp_fusion), kind=kCustom, calls=%fused_computation.4 | custom fusion | bytes 98304 | tf_op jit(solution)/shard_map/gather | solution.py:220
  1398.0 4.6 all-to-all-start.4
  1404.5 3.6 collective-permute-start.19
  1408.2 10.7 copy.60
  1418.9 43.2 %scatter_custom_fusion.5 = f32[32768]{0:T(1024)S(1)} fusion(s32[8192]{0:T(1024)S(1)} %bitcast.1554, f32[8192]{0:T(1024)S(1)} %mul.1284, f32[]{:T(128)} %constant.128.clone.1), kind=kCustom, calls=%fused_computation.226 | custom fusion | flops 8192 | bytes 131076 | tf_op jit(solution)/shard_map/scatter-add | solution.py:227
  (238 shorter events, 101.0 us)
Async XLA Ops:
  0.6 66.2 %copy-start = (f32[4,64,128]{2,1,0:T(8,128)S(1)}, f32[4,64,128]{2,1,0:T(8,128)}, u32[]{:S(2)}) copy-start(f32[4,64,128]{2,1,0:T(8,128)} %param.14) | copy-start | bytes 393220
  0.6 68.8 %copy-start.1 = (f32[2,4,64,128]{3,2,1,0:T(8,128)S(1)}, f32[2,4,64,128]{3,2,1,0:T(8,128)}, u32[]{:S(2)}) copy-start(f32[2,4,64,128]{3,2,1,0:T(8,128)} %param.15) | copy-start | bytes 786436
  0.7 66.3 %copy-start.2 = (s32[4,64,128]{2,1,0:T(8,128)S(1)}, s32[4,64,128]{2,1,0:T(8,128)}, u32[]{:S(2)}) copy-start(s32[4,64,128]{2,1,0:T(8,128)} %param.19) | copy-start | bytes 393220
  0.7 67.0 %copy-start.9 = (s32[1,1,8]{2,1,0:T(1,128)S(1)}, s32[1,1,8]{2,1,0:T(1,128)}, u32[]{:S(2)}) copy-start(s32[1,1,8]{2,1,0:T(1,128)} %param.21) | copy-start | bytes 100
  7.3 80.2 %collective-permute-start = (f32[7,1,64,128]{3,2,1,0:T(8,128)}, f32[7,1,64,128]{3,2,1,0:T(8,128)S(1)}, u32[]{:S(2)}, u32[]{:S(2)}) collective-permute-start(f32[7,1,64,128]{3,2,1,0:T(8,128)} %get-tuple-element.466), channel_id=1, source_target_pairs={{0,1},{1,2},{2,3},{3,4},{4,5},{5,6},{6,7},{7,8},{8,9},{9,10},{10,1... | collective-permute-start | bytes 688136 | tf_op jit(solution)/shard_map/ppermute | solution.py:22
  11.7 75.8 %collective-permute-start.1 = (f32[7,1,64,128]{3,2,1,0:T(8,128)}, f32[7,1,64,128]{3,2,1,0:T(8,128)S(1)}, u32[]{:S(2)}, u32[]{:S(2)}) collective-permute-start(f32[7,1,64,128]{3,2,1,0:T(8,128)} %get-tuple-element.467), channel_id=1, source_target_pairs={{1,0},{2,1},{3,2},{4,3},{5,4},{6,5},{7,6},{8,7},{9,8},{10,9},{11,1... | collective-permute-start | bytes 688136 | tf_op jit(solution)/shard_map/ppermute | solution.py:24
  60.6 23.3 %all-to-all-start = ((f32[4,8,1024]{2,0,1:T(4,128)}), f32[4,8,1024]{2,0,1:T(4,128)S(1)}, u32[]{:S(2)}, u32[]{:S(2)}) async-start(f32[4,8,1024]{2,0,1:T(4,128)} %copy.52), calls=%async_computation | async-start | bytes 262144 | tf_op jit(solution)/shard_map/all_to_all | solution.py:178
  87.5 5.5 collective-permute-start.2
  91.0 5.1 collective-permute-start.3
  158.3 27.1 %copy-start.3 = (f32[4,64,128]{2,1,0:T(8,128)S(1)}, f32[4,64,128]{2,1,0:T(8,128)}, u32[]{:S(2)}) copy-start(f32[4,64,128]{2,1,0:T(8,128)} %get-tuple-element.259) | copy-start | bytes 393220
  158.3 27.2 %copy-start.7 = (f32[3,8,1024]{2,0,1:T(4,128)S(1)}, f32[3,8,1024]{2,0,1:T(4,128)}, u32[]{:S(2)}) copy-start(f32[3,8,1024]{2,0,1:T(4,128)} %get-tuple-element.265) | copy-start | bytes 294916
  835.1 105.3 %collective-permute-start.4 = (f32[1,64,128]{2,1,0:T(8,128)S(1)}, f32[1,64,128]{2,1,0:T(8,128)S(1)}, u32[]{:S(2)}, u32[]{:S(2)}) collective-permute-start(f32[1,64,128]{2,1,0:T(8,128)S(1)} %broadcast_in_dim.915), channel_id=1, source_target_pairs={{1,0},{2,1},{3,2},{4,3},{5,4},{6,5},{7,6},{8,7},{9,8},{10,9},{11,1... | collective-permute-start | bytes 98312 | tf_op jit(solution)/shard_map/ppermute | solution.py:24
  837.1 103.4 %collective-permute-start.5 = (f32[1,64,128]{2,1,0:T(8,128)S(1)}, f32[1,64,128]{2,1,0:T(8,128)S(1)}, u32[]{:S(2)}, u32[]{:S(2)}) collective-permute-start(f32[1,64,128]{2,1,0:T(8,128)S(1)} %broadcast_in_dim.916), channel_id=1, source_target_pairs={{0,1},{1,2},{2,3},{3,4},{4,5},{5,6},{6,7},{7,8},{8,9},{9,10},{10,1... | collective-permute-start | bytes 98312 | tf_op jit(solution)/shard_map/ppermute | solution.py:22
  841.2 104.8 %copy-start.8 = (f32[1,1,8,1024]{3,2,1,0:T(8,128)S(1)}, f32[1,1,8,1024]{3,2,1,0:T(8,128)}, u32[]{:S(2)}) copy-start(f32[1,1,8,1024]{3,2,1,0:T(8,128)} %param.22) | copy-start | bytes 98308
  921.8 24.2 %all-to-all-start.1 = ((f32[8,1,1024]{2,1,0:T(1,128)}), f32[8,1,1024]{2,1,0:T(1,128)S(1)}, u32[]{:S(2)}, u32[]{:S(2)}) async-start(f32[8,1,1024]{2,1,0:T(1,128)} %bitcast.697), calls=%async_computation.1 | async-start | bytes 65536 | tf_op jit(solution)/shard_map/all_to_all | solution.py:221
  940.5 93.4 %collective-permute-start.6 = (f32[6,1,128]{2,1,0:T(1,128)S(1)}, f32[6,1,128]{2,1,0:T(1,128)S(1)}, u32[]{:S(2)}, u32[]{:S(2)}) collective-permute-start(f32[6,1,128]{2,1,0:T(1,128)S(1)} %get-tuple-element.489), channel_id=1, source_target_pairs={{32,0},{64,32},{96,64},{128,96},{160,128},{192,160},{224,192},{33,... | collective-permute-start | bytes 9224 | tf_op jit(solution)/shard_map/ppermute | solution.py:24
  942.5 91.4 %collective-permute-start.7 = (f32[6,1,128]{2,1,0:T(1,128)S(1)}, f32[6,1,128]{2,1,0:T(1,128)S(1)}, u32[]{:S(2)}, u32[]{:S(2)}) collective-permute-start(f32[6,1,128]{2,1,0:T(1,128)S(1)} %get-tuple-element.490), channel_id=1, source_target_pairs={{0,32},{32,64},{64,96},{96,128},{128,160},{160,192},{192,224},{1,3... | collective-permute-start | bytes 9224 | tf_op jit(solution)/shard_map/ppermute | solution.py:22
  1034.1 88.9 %collective-permute-start.9 = (f32[1,64,128]{2,1,0:T(8,128)S(1)}, f32[1,64,128]{2,1,0:T(8,128)S(1)}, u32[]{:S(2)}, u32[]{:S(2)}) collective-permute-start(f32[1,64,128]{2,1,0:T(8,128)S(1)} %get-tuple-element.497), channel_id=1, source_target_pairs={{0,1},{1,2},{2,3},{3,4},{4,5},{5,6},{6,7},{7,8},{8,9},{9,10},{10,1... | collective-permute-start | bytes 98312 | tf_op jit(solution)/shard_map/ppermute | solution.py:22
  1036.6 86.5 %collective-permute-start.8 = (f32[1,64,128]{2,1,0:T(8,128)S(1)}, f32[1,64,128]{2,1,0:T(8,128)S(1)}, u32[]{:S(2)}, u32[]{:S(2)}) collective-permute-start(f32[1,64,128]{2,1,0:T(8,128)S(1)} %get-tuple-element.498), channel_id=1, source_target_pairs={{1,0},{2,1},{3,2},{4,3},{5,4},{6,5},{7,6},{8,7},{9,8},{10,9},{11,1... | collective-permute-start | bytes 98312 | tf_op jit(solution)/shard_map/ppermute | solution.py:24
  1118.4 10.2 all-to-all-start.2
  1123.0 48.9 %collective-permute-start.10 = (f32[6,1,128]{2,1,0:T(1,128)S(1)}, f32[6,1,128]{2,1,0:T(1,128)S(1)}, u32[]{:S(2)}, u32[]{:S(2)}) collective-permute-start(f32[6,1,128]{2,1,0:T(1,128)S(1)} %get-tuple-element.487), channel_id=1, source_target_pairs={{32,0},{64,32},{96,64},{128,96},{160,128},{192,160},{224,192},{33,... | collective-permute-start | bytes 9224 | tf_op jit(solution)/shard_map/ppermute | solution.py:24
  1125.0 46.9 %collective-permute-start.11 = (f32[6,1,128]{2,1,0:T(1,128)S(1)}, f32[6,1,128]{2,1,0:T(1,128)S(1)}, u32[]{:S(2)}, u32[]{:S(2)}) collective-permute-start(f32[6,1,128]{2,1,0:T(1,128)S(1)} %get-tuple-element.488), channel_id=1, source_target_pairs={{0,32},{32,64},{64,96},{96,128},{128,160},{160,192},{192,224},{1,3... | collective-permute-start | bytes 9224 | tf_op jit(solution)/shard_map/ppermute | solution.py:22
  1172.1 90.7 %collective-permute-start.13 = (f32[1,64,128]{2,1,0:T(8,128)S(1)}, f32[1,64,128]{2,1,0:T(8,128)S(1)}, u32[]{:S(2)}, u32[]{:S(2)}) collective-permute-start(f32[1,64,128]{2,1,0:T(8,128)S(1)} %get-tuple-element.495), channel_id=1, source_target_pairs={{0,1},{1,2},{2,3},{3,4},{4,5},{5,6},{6,7},{7,8},{8,9},{9,10},{10,1... | collective-permute-start | bytes 98312 | tf_op jit(solution)/shard_map/ppermute | solution.py:22
  1176.4 86.4 %collective-permute-start.12 = (f32[1,64,128]{2,1,0:T(8,128)S(1)}, f32[1,64,128]{2,1,0:T(8,128)S(1)}, u32[]{:S(2)}, u32[]{:S(2)}) collective-permute-start(f32[1,64,128]{2,1,0:T(8,128)S(1)} %get-tuple-element.496), channel_id=1, source_target_pairs={{1,0},{2,1},{3,2},{4,3},{5,4},{6,5},{7,6},{8,7},{9,8},{10,9},{11,1... | collective-permute-start | bytes 98312 | tf_op jit(solution)/shard_map/ppermute | solution.py:24
  1258.3 10.2 all-to-all-start.3
  1262.9 48.9 %collective-permute-start.14 = (f32[6,1,128]{2,1,0:T(1,128)S(1)}, f32[6,1,128]{2,1,0:T(1,128)S(1)}, u32[]{:S(2)}, u32[]{:S(2)}) collective-permute-start(f32[6,1,128]{2,1,0:T(1,128)S(1)} %get-tuple-element.485), channel_id=1, source_target_pairs={{32,0},{64,32},{96,64},{128,96},{160,128},{192,160},{224,192},{33,... | collective-permute-start | bytes 9224 | tf_op jit(solution)/shard_map/ppermute | solution.py:24
  1264.8 46.9 %collective-permute-start.15 = (f32[6,1,128]{2,1,0:T(1,128)S(1)}, f32[6,1,128]{2,1,0:T(1,128)S(1)}, u32[]{:S(2)}, u32[]{:S(2)}) collective-permute-start(f32[6,1,128]{2,1,0:T(1,128)S(1)} %get-tuple-element.486), channel_id=1, source_target_pairs={{0,32},{32,64},{64,96},{96,128},{128,160},{160,192},{192,224},{1,3... | collective-permute-start | bytes 9224 | tf_op jit(solution)/shard_map/ppermute | solution.py:22
  1311.9 90.7 %collective-permute-start.17 = (f32[1,64,128]{2,1,0:T(8,128)S(1)}, f32[1,64,128]{2,1,0:T(8,128)S(1)}, u32[]{:S(2)}, u32[]{:S(2)}) collective-permute-start(f32[1,64,128]{2,1,0:T(8,128)S(1)} %get-tuple-element.493), channel_id=1, source_target_pairs={{0,1},{1,2},{2,3},{3,4},{4,5},{5,6},{6,7},{7,8},{8,9},{9,10},{10,1... | collective-permute-start | bytes 98312 | tf_op jit(solution)/shard_map/ppermute | solution.py:22
  1316.2 86.4 %collective-permute-start.16 = (f32[1,64,128]{2,1,0:T(8,128)S(1)}, f32[1,64,128]{2,1,0:T(8,128)S(1)}, u32[]{:S(2)}, u32[]{:S(2)}) collective-permute-start(f32[1,64,128]{2,1,0:T(8,128)S(1)} %get-tuple-element.494), channel_id=1, source_target_pairs={{1,0},{2,1},{3,2},{4,3},{5,4},{6,5},{7,6},{8,7},{9,8},{10,9},{11,1... | collective-permute-start | bytes 98312 | tf_op jit(solution)/shard_map/ppermute | solution.py:24
  1398.0 20.8 %all-to-all-start.4 = ((f32[8,1,1024]{2,1,0:T(1,128)}), f32[8,1,1024]{2,1,0:T(1,128)S(1)}, u32[]{:S(2)}, u32[]{:S(2)}) async-start(f32[8,1,1024]{2,1,0:T(1,128)} %bitcast.709), calls=%async_computation.4 | async-start | bytes 65536 | tf_op jit(solution)/shard_map/all_to_all | solution.py:221
  1402.6 59.5 %collective-permute-start.18 = (f32[6,1,128]{2,1,0:T(1,128)S(1)}, f32[6,1,128]{2,1,0:T(1,128)S(1)}, u32[]{:S(2)}, u32[]{:S(2)}) collective-permute-start(f32[6,1,128]{2,1,0:T(1,128)S(1)} %get-tuple-element.483), channel_id=1, source_target_pairs={{32,0},{64,32},{96,64},{128,96},{160,128},{192,160},{224,192},{33,... | collective-permute-start | bytes 9224 | tf_op jit(solution)/shard_map/ppermute | solution.py:24
  1404.5 57.6 %collective-permute-start.19 = (f32[6,1,128]{2,1,0:T(1,128)S(1)}, f32[6,1,128]{2,1,0:T(1,128)S(1)}, u32[]{:S(2)}, u32[]{:S(2)}) collective-permute-start(f32[6,1,128]{2,1,0:T(1,128)S(1)} %get-tuple-element.484), channel_id=1, source_target_pairs={{0,32},{32,64},{64,96},{96,128},{128,160},{160,192},{192,224},{1,3... | collective-permute-start | bytes 9224 | tf_op jit(solution)/shard_map/ppermute | solution.py:22
  (3 other events, 48.0 us)
where the time goes:
time: 1480 us; the launch traced here: 1460 us
  local copies, waits for them, and re-layouts  445 us (30%)
  loops' own time  420 us (28%)
  other arithmetic  311 us (21%)
  between operations  141 us (10%)
  starting transfers between devices  91 us (6%)
  blocking collectives  51.3 us (3%)
    another operation x2, loops' own time, coarse_solve(): lax.linalg.tridiagonal_solve(-below, diagonal, upper, source[:, None])[:, 0]  420 us
    gather x4, local copies, waits for them, and re-layouts, body(): update.reshape(-1)[flat_index].reshape(sector_count, slot_count)  322 us
    scatter-add x4, other arithmetic, body(): extra = jnp.zeros((layer_count * row_count * column_count,), jnp.float32)...  173 us
    scatter-add x1, other arithmetic, body(): residual = residual.reshape(3, -1).at[:, flat_index].add(fault_flux.resha...  51.4 us
    scatter-add x1, other arithmetic, body(): diagonal.reshape(-1).at[flat_index].add(fault_link.reshape(-1))  44.3 us
    all_gather x1, blocking collectives, body(): coarse_rows = lax.all_gather(summed, 'slab', axis=1, tiled=True)  40.8 us
    ppermute x10, starting transfers between devices, padded_2(): lax.ppermute(tail, axis, [(i, (i + 1) % count) for i in range(ends)])  37.3 us
    slice x54, local copies, waits for them, and re-layouts, coarse_solve(): lax.linalg.tridiagonal_solve(-below, diagonal, upper, source[:, None])[:, 0]  34.7 us
  transfers between devices with their start and end apart: 25, of which 1 were waited for; matrix products, arithmetic and copies ran while one was open for 42% of the time, Pallas kernels for 0%

commit v1 on v0

v1 whole, which is shorter than its diff:
```python
import functools

import jax
import jax.numpy as jnp
from jax import lax
from jax.experimental import pallas as pl
from jax.experimental.pallas import tpu as pltpu
from jax.sharding import PartitionSpec as P

COMPRESS = (0.0002, 0.0005, 0.002)
VISCOSITY = (1.0, 3.0, 0.5)
RELAXATION = 2.0 / 3.0
SWEEPS = 4

BF = jnp.bfloat16
F32 = jnp.float32
MESH = pl.DeviceIdType.MESH

LAYERS, ROWS, COLS = 4, 64, 128
CELLS_HI = LAYERS * ROWS
SLOTS = 1024
CHUNKS = SLOTS // 128


def split(value, count):
    parts = []
    for _ in range(count - 1):
        part = value.astype(BF)
        parts.append(part)
        value = value - part.astype(F32)
    parts.append(value.astype(BF))
    return parts


def mobilities(s_water, s_gas):
    s_oil = 1.0 - s_water - s_gas
    return [s * s * (1.0 / v) for s, v in zip((s_water, s_oil, s_gas), VISCOSITY)]


def face(p_low, m_low, weight, words, p_high, m_high, first_bit):
    drop = p_low - p_high
    fluxes, total = [], None
    for a in range(3):
        flag = jnp.bitwise_and(words, 1 << (first_bit + a)) != 0
        part = weight * jnp.where(flag, m_low[a], m_high[a])
        fluxes.append(part * drop)
        total = part if total is None else total + part
    return fluxes, total


def kernel(
    n_sector, n_slab,
    p_ref, s_ref, om_ref, pv_ref, tr_ref, bits_ref, fc_ref, cnt_ref, ft_ref, fu_ref,
    res_ref, out_ref, *,
    oh, ohlo, fsplit, acc, cell, fweight, fup, own, far, link, vals,
    up_stage, dn_stage, halo_lo, halo_hi, rup_stage, rdn_stage, rhalo_lo, rhalo_hi,
    asend, arecv, bsend, brecv,
    cz, cxu, cxd, cyu, cyd, storage, rhs, inv, ubuf, part,
    uown, urecv, usend, zlo, zhi, xup, xdn, xlo, xhi,
    f_ss, f_rs, h_ss, h_rs, a_ss, a_rs, b_ss, b_rs, u_ss, u_rs, w_ss, w_rs,
):
    me = lax.axis_index("sector")
    t = lax.axis_index("slab")
    others = n_sector - 1
    s_next = lax.rem(me + 1, n_sector)
    s_prev = lax.rem(me + n_sector - 1, n_sector)
    t_next = lax.rem(t + 1, n_slab)
    t_prev = lax.rem(t + n_slab - 1, n_slab)

    def copy(src, dst, ss, rs, device):
        return pltpu.make_async_remote_copy(
            src_ref=src, dst_ref=dst, send_sem=ss, recv_sem=rs,
            device_id=device, device_id_type=MESH,
        )

    def sector_of(d):
        return lax.rem(me + d, n_sector)

    barrier = pltpu.get_barrier_semaphore()

    @pl.loop(1, n_sector)
    def _(d):
        pl.semaphore_signal(barrier, inc=1, device_id=(sector_of(d), t), device_id_type=MESH)

    @pl.loop(1, n_slab)
    def _(k):
        pl.semaphore_signal(
            barrier, inc=1, device_id=(me, lax.rem(t + k, n_slab)), device_id_type=MESH
        )

    top = LAYERS - 1
    for i, plane in enumerate((p_ref[top], s_ref[0, top], s_ref[1, top], tr_ref[0, top])):
        up_stage[i] = plane
    up_stage[4] = bits_ref[top].astype(F32)
    for i, plane in enumerate((p_ref[0], s_ref[0, 0], s_ref[1, 0])):
        dn_stage[i] = plane
    last = ROWS - 1
    for k in range(LAYERS):
        for i, row in enumerate(
            (p_ref[k, last:], s_ref[0, k, last:], s_ref[1, k, last:], tr_ref[1, k, last:])
        ):
            rup_stage[i, k : k + 1, :] = row
        rup_stage[4, k : k + 1, :] = bits_ref[k, last:].astype(F32)
        for i, row in enumerate((p_ref[k, :1], s_ref[0, k, :1], s_ref[1, k, :1])):
            rdn_stage[i, k : k + 1, :] = row

    lane = lax.broadcasted_iota(jnp.int32, (1, 128), 1)
    counts = [cnt_ref[0, 0, sector_of(d)] for d in range(1, n_sector)]
    turn = lax.rem(n_sector - me, n_sector)
    for b in range(CHUNKS):
        span = slice(b * 128, (b + 1) * 128)
        cells = pltpu.roll(fc_ref[0, 0, :, span], turn, 0)
        flags = pltpu.roll(fu_ref[0, 0, :, span], turn, 0)
        trans = pltpu.roll(ft_ref[0, 0, :, span], turn, 0)
        for d in range(others):
            row = slice(d + 1, d + 2)
            cell[d, b : b + 1, :] = cells[row]
            fup[d, b : b + 1, :] = flags[row]
            fweight[d, b : b + 1, :] = jnp.where(lane + b * 128 < counts[d], trans[row], 0.0)

    for i, field in enumerate((p_ref, s_ref.at[0], s_ref.at[1])):
        flipped = field[...].reshape(CELLS_HI, COLS).T
        for j, piece in enumerate(split(flipped, 3)):
            fsplit[i, j * 128 : (j + 1) * 128, :] = piece

    sub = lax.broadcasted_iota(jnp.int32, (128, 128), 0)
    sub_hi = lax.broadcasted_iota(jnp.int32, (CELLS_HI, 128), 0)

    @pl.loop(0, others)
    def _(d):
        for b in range(CHUNKS):
            span = slice(b * 128, (b + 1) * 128)
            c = cell[d, b : b + 1, :]
            oh[d, :, span] = jnp.where(sub_hi == jnp.right_shift(c, 7), 1.0, 0.0).astype(BF)
            ohlo[d, :, span] = jnp.where(sub == jnp.bitwise_and(c, 127), 1.0, 0.0).astype(BF)

    pl.semaphore_wait(barrier, n_sector - 1 + n_slab - 1)

    halo_copies = [
        copy(up_stage, halo_lo, h_ss.at[0], h_rs.at[0], (me, t_next)),
        copy(dn_stage, halo_hi, h_ss.at[1], h_rs.at[1], (me, t_prev)),
        copy(rup_stage, rhalo_lo, h_ss.at[2], h_rs.at[2], (s_next, t)),
        copy(rdn_stage, rhalo_hi, h_ss.at[3], h_rs.at[3], (s_prev, t)),
    ]
    for c in halo_copies:
        c.start()

    def gather(d, weights, count, store):
        for b in range(CHUNKS // 2):
            picks = oh[d, :, b * 256 : (b + 1) * 256]
            rows = [jnp.bitwise_and(cell[d, 2 * b + k : 2 * b + k + 1, :], 127) for k in range(2)]
            for i, w in enumerate(weights):
                g = jnp.dot(w, picks, preferred_element_type=F32)
                total = g[(count - 1) * 128 :]
                for j in reversed(range(count - 1)):
                    total = g[j * 128 : (j + 1) * 128] + total
                for k in range(2):
                    found = jnp.where(sub == rows[k], total[:, k * 128 : (k + 1) * 128], 0.0)
                    store(i, 2 * b + k, jnp.sum(found, axis=0, keepdims=True))

    def fault_copy(d):
        return copy(own.at[d], far.at[others - 1 - d], f_ss.at[d], f_rs.at[others - 1 - d],
                    (sector_of(d + 1), t))

    @pl.loop(0, others)
    def _(d):
        def store(i, b, row):
            own[d, i, pl.ds(b, 1), :] = row

        gather(d, [fsplit[i] for i in range(3)], 3, store)
        own[d, 3] = jnp.right_shift(cell[d], 13).astype(F32)
        fault_copy(d).start()

    lane2 = lax.broadcasted_iota(jnp.int32, (ROWS, COLS), 1)
    row2 = lax.broadcasted_iota(jnp.int32, (ROWS, COLS), 0)
    not_first_slab = jnp.where(t > 0, 1.0, 0.0).astype(F32)
    not_last_slab = jnp.where(t < n_slab - 1, 1.0, 0.0).astype(F32)
    not_first_sector = jnp.where(me > 0, 1.0, 0.0).astype(F32)
    not_last_sector = jnp.where(me < n_sector - 1, 1.0, 0.0).astype(F32)

    for k in range(LAYERS):
        p = p_ref[k]
        pv = pv_ref[k]
        sw, sg = s_ref[0, k], s_ref[1, k]
        so = 1.0 - sw - sg
        m = mobilities(sw, sg)
        words = bits_ref[k]
        sat = (sw, so, sg)
        st = pv * (sw * COMPRESS[0] + so * COMPRESS[1] + sg * COMPRESS[2])
        storage[k] = st
        res = [pv * sat[a] * (1.0 + COMPRESS[a] * p) - om_ref[a, k] for a in range(3)]
        flux, coupling = face(
            p, m, jnp.where(lane2 < COLS - 1, tr_ref[2, k], 0.0), words,
            pltpu.roll(p, COLS - 1, 1), [pltpu.roll(x, COLS - 1, 1) for x in m], 6,
        )
        res = [res[a] + (flux[a] - pltpu.roll(flux[a], 1, 1)) for a in range(3)]
        back = pltpu.roll(coupling, 1, 1)
        cyu[k] = coupling
        cyd[k] = back
        inv[k] = st + (coupling + back)
        for a in range(3):
            res_ref[a, k] = res[a]
        if k > 0:
            flux, coupling = face(
                p_ref[k - 1], mobilities(s_ref[0, k - 1], s_ref[1, k - 1]), tr_ref[0, k - 1],
                bits_ref[k - 1], p, m, 0,
            )
            cz[k] = coupling
            inv[k] += coupling
            inv[k - 1] += coupling
            for a in range(3):
                res_ref[a, k] -= flux[a]
                res_ref[a, k - 1] += flux[a]

    for c in halo_copies:
        c.wait_recv()

    p = p_ref[0]
    m = mobilities(s_ref[0, 0], s_ref[1, 0])
    flux, coupling = face(
        halo_lo[0], mobilities(halo_lo[1], halo_lo[2]), halo_lo[3] * not_first_slab,
        halo_lo[4].astype(jnp.int32), p, m, 0,
    )
    cz[0] = coupling
    inv[0] += coupling
    for a in range(3):
        res_ref[a, 0] -= flux[a]
    p = p_ref[top]
    m = mobilities(s_ref[0, top], s_ref[1, top])
    flux, coupling = face(
        p, m, tr_ref[0, top] * not_last_slab, bits_ref[top],
        halo_hi[0], mobilities(halo_hi[1], halo_hi[2]), 0,
    )
    cz[LAYERS] = coupling
    inv[top] += coupling
    for a in range(3):
        res_ref[a, top] += flux[a]

    first_p = rdn_stage[0]
    low_flux, low_link = face(
        rhalo_lo[0], mobilities(rhalo_lo[1], rhalo_lo[2]), rhalo_lo[3] * not_first_sector,
        rhalo_lo[4].astype(jnp.int32), first_p, mobilities(rdn_stage[1], rdn_stage[2]), 3,
    )
    hi_m = mobilities(rhalo_hi[1], rhalo_hi[2])
    for k in range(LAYERS):
        p = p_ref[k]
        m = mobilities(s_ref[0, k], s_ref[1, k])

        def after(x, edge):
            return jnp.where(row2 == last, edge[k : k + 1], pltpu.roll(x, last, 0))

        def before(x, edge):
            return jnp.where(row2 == 0, edge[k : k + 1], pltpu.roll(x, 1, 0))

        weight = tr_ref[1, k] * jnp.where(row2 == last, not_last_sector, 1.0)
        flux, coupling = face(
            p, m, weight, bits_ref[k], after(p, rhalo_hi[0]),
            [after(m[a], hi_m[a]) for a in range(3)], 3,
        )
        back = before(coupling, low_link)
        cxu[k] = coupling
        cxd[k] = back
        inv[k] += coupling + back
        for a in range(3):
            res_ref[a, k] += flux[a] - before(flux[a], low_flux[a])

    zero_tile = jnp.zeros((CHUNKS, 128), F32)
    layer_source = [zero_tile] * LAYERS
    for d in range(others):
        fault_copy(others - 1 - d).wait_recv()
        flags = fup[d]
        w = fweight[d]
        flux, coupling = face(
            own[d, 0], mobilities(own[d, 1], own[d, 2]), w, flags,
            far[d, 0], mobilities(far[d, 1], far[d, 2]), 0,
        )
        for a in range(3):
            vals[d, a] = flux[a]
        vals[d, 3] = coupling
        link[d] = coupling
        layer = jnp.right_shift(cell[d], 13)
        total = flux[0] + flux[1] + flux[2]
        for k in range(LAYERS):
            layer_source[k] = layer_source[k] - jnp.where(layer == k, total, 0.0)

    for k in range(LAYERS):
        regular = -(res_ref[0, k] + res_ref[1, k] + res_ref[2, k])
        source = jnp.sum(regular, axis=0, keepdims=True) + jnp.sum(
            layer_source[k], axis=0, keepdims=True
        )
        asend[k : k + 1, :] = jnp.sum(storage[k], axis=0, keepdims=True)
        asend[4 + k : 5 + k, :] = jnp.sum(cz[k + 1], axis=0, keepdims=True)
        asend[8 + k : 9 + k, :] = source
    asend[12:16, :] = jnp.zeros((4, 128), F32)

    def a_copy(d):
        return copy(asend, arecv.at[others - 1 - d], a_ss.at[d], a_rs.at[others - 1 - d],
                    (sector_of(d + 1), t))

    @pl.loop(0, others)
    def _(d):
        a_copy(d).start()

    def masked(d, field, count):
        pieces = []
        for b in range(CHUNKS):
            value = field[b : b + 1, :]
            mask = ohlo[d, :, b * 128 : (b + 1) * 128]
            pieces.append(jnp.concatenate([mask * x for x in split(value, count)], 0))
        return jnp.concatenate(pieces, 1)

    nt = (((1,), (1,)), ((), ()))
    acc[...] = jnp.zeros(acc.shape, F32)

    @pl.loop(0, others)
    def _(d):
        for i in range(4):
            acc[i] += lax.dot_general(
                masked(d, vals.at[d, i], 3), oh[d], nt, preferred_element_type=F32
            )

    def unfold(total):
        return total.T.reshape(LAYERS, ROWS, COLS)

    for i in range(4):
        placed = unfold(acc[i, :128] + (acc[i, 128:256] + acc[i, 256:]))
        if i < 3:
            res_ref[i] += placed
        else:
            inv[...] = RELAXATION / (inv[...] + placed)
    for k in range(LAYERS):
        rhs[k] = -(res_ref[0, k] + res_ref[1, k] + res_ref[2, k])

    sums = asend[...]
    for d in range(others):
        a_copy(others - 1 - d).wait_recv()
        sums = sums + arecv[d]
    column = jnp.sum(sums, axis=1, keepdims=True)
    lane16 = lax.broadcasted_iota(jnp.int32, (16, 128), 1)
    row16 = lax.broadcasted_iota(jnp.int32, (16, 128), 0)
    spread = jnp.where(
        jnp.bitwise_and(lane16, 3) == jnp.bitwise_and(row16, 3), jnp.broadcast_to(column, (16, 128)), 0.0
    )
    for q in range(4):
        bsend[q : q + 1, :] = jnp.sum(spread[4 * q : 4 * q + 4], axis=0, keepdims=True)
    brecv[t] = bsend[...]

    def b_copy(k, dst):
        return copy(bsend, brecv.at[dst], b_ss.at[k - 1], b_rs.at[k - 1],
                    (me, lax.rem(t + k, n_slab)))

    @pl.loop(1, n_slab)
    def _(k):
        b_copy(k, t).start()

    @pl.loop(1, n_slab)
    def _(k):
        b_copy(k, lax.rem(t + n_slab - k, n_slab)).wait_recv()

    lane4 = lax.broadcasted_iota(jnp.int32, (4, 128), 1)
    rows = jnp.zeros((4, 128), F32)
    for j in range(n_slab):
        rows = rows + jnp.where(jnp.right_shift(lane4, 2) == j, brecv[j], 0.0)
    s_row, right, rhs_row = rows[0:1], rows[1:2], rows[2:3]
    lane1 = lax.broadcasted_iota(jnp.int32, (1, 128), 1)
    right = jnp.where(lane1 < LAYERS * n_slab - 1, right, 0.0)
    s_row = jnp.where(lane1 < LAYERS * n_slab, s_row, 1.0)
    left = jnp.where(lane1 > 0, pltpu.roll(right, 1, 1), 0.0)
    step = 1
    while step < LAYERS * n_slab:
        pivot = 1.0 / (s_row + left + right)
        sn, ln, rn, dn = s_row * pivot, left * pivot, right * pivot, rhs_row * pivot
        s_row = s_row + left * pltpu.roll(sn, step, 1) + right * pltpu.roll(sn, 128 - step, 1)
        rhs_row = rhs_row + left * pltpu.roll(dn, step, 1) + right * pltpu.roll(dn, 128 - step, 1)
        left = left * pltpu.roll(ln, step, 1)
        right = right * pltpu.roll(rn, 128 - step, 1)
        step *= 2
    coarse = rhs_row / s_row
    lane8 = lax.broadcasted_iota(jnp.int32, (8, 128), 1)
    row8 = lax.broadcasted_iota(jnp.int32, (8, 128), 0)
    level = jnp.sum(
        jnp.where(lane8 == row8 + (LAYERS * t - 1), jnp.broadcast_to(coarse, (8, 128)), 0.0),
        axis=1, keepdims=True,
    )
    level = jnp.broadcast_to(level, (8, 128))

    def level_row(k):
        return level[k + 1 : k + 2]

    def fault_extra(value_of):
        def body(d, total):
            vals[d, 0] = link[d] * value_of(d)
            return total + lax.dot_general(
                masked(d, vals.at[d, 0], 2), oh[d], nt, preferred_element_type=F32
            )

        total = lax.fori_loop(0, others, body, jnp.zeros((256, 256), F32))
        return unfold(total[:128] + total[128:])

    def coarse_far(d):
        value = zero_tile
        for k in range(LAYERS):
            value = jnp.where(far[d, 3] == k, level_row(k), value)
        return value

    part[...] = fault_extra(coarse_far)
    for k in range(LAYERS):
        here = level_row(k)
        total = part[k] + rhs[k] + cz[k + 1] * level_row(k + 1) + cz[k] * level_row(k - 1)
        total = total + (cxu[k] + cxd[k] + cyu[k] + cyd[k]) * here
        ubuf[k] = (1.0 - RELAXATION) * here + inv[k] * total

    sends = []
    for sweep in range(SWEEPS - 1):
        for k in range(LAYERS):
            xup[sweep, k : k + 1, :] = ubuf[k, last:]
            xdn[sweep, k : k + 1, :] = ubuf[k, :1]
        usend[sweep, 0] = ubuf[top]
        usend[sweep, 1] = ubuf[0]
        edge_copies = [
            copy(usend.at[sweep, 0], zlo.at[sweep], w_ss.at[sweep, 0], w_rs.at[sweep, 0], (me, t_next)),
            copy(usend.at[sweep, 1], zhi.at[sweep], w_ss.at[sweep, 1], w_rs.at[sweep, 1], (me, t_prev)),
            copy(xup.at[sweep], xlo.at[sweep], w_ss.at[sweep, 2], w_rs.at[sweep, 2], (s_next, t)),
            copy(xdn.at[sweep], xhi.at[sweep], w_ss.at[sweep, 3], w_rs.at[sweep, 3], (s_prev, t)),
        ]
        for c in edge_copies:
            c.start()
        sends += edge_copies
        flipped = ubuf[...].reshape(CELLS_HI, COLS).T
        weights = jnp.concatenate(split(flipped, 2), 0)
        fsplit[0, :256, :] = weights

        def u_copy(d, sweep=sweep):
            return copy(
                uown.at[sweep, d], urecv.at[sweep, others - 1 - d],
                u_ss.at[sweep, d], u_rs.at[sweep, others - 1 - d], (sector_of(d + 1), t),
            )

        @pl.loop(0, others)
        def _(d, sweep=sweep, u_copy=u_copy):
            def store(i, b, row):
                uown[sweep, d, pl.ds(b, 1), :] = row

            gather(d, [fsplit[0, :256]], 2, store)
            u_copy(d).start()

        for k in range(LAYERS):
            u = ubuf[k]
            total = rhs[k] + cyu[k] * pltpu.roll(u, COLS - 1, 1) + cyd[k] * pltpu.roll(u, 1, 1)
            total = total + cxu[k] * jnp.where(row2 == last, 0.0, pltpu.roll(u, last, 0))
            total = total + cxd[k] * jnp.where(row2 == 0, 0.0, pltpu.roll(u, 1, 0))
            if k > 0:
                total = total + cz[k] * ubuf[k - 1]
            if k < top:
                total = total + cz[k + 1] * ubuf[k + 1]
            part[k] = total
        for c in edge_copies:
            c.wait_recv()
        part[0] += cz[0] * zlo[sweep]
        part[top] += cz[LAYERS] * zhi[sweep]
        for k in range(LAYERS):
            part[k, last:] += cxu[k, last:] * xhi[sweep, k : k + 1, :]
            part[k, :1] += cxd[k, :1] * xlo[sweep, k : k + 1, :]
        for d in range(others):
            u_copy(others - 1 - d).wait_recv()
        target = out_ref if sweep == SWEEPS - 2 else ubuf
        extra = fault_extra(lambda d, sweep=sweep: urecv[sweep, d])
        for k in range(LAYERS):
            target[k] = (1.0 - RELAXATION) * ubuf[k] + inv[k] * (part[k] + extra[k])

    for c in halo_copies + sends:
        c.wait_send()
    for d in range(others):
        fault_copy(d).wait_send()
        a_copy(d).wait_send()
        for sweep in range(SWEEPS - 1):
            copy(
                uown.at[sweep, d], urecv.at[sweep, others - 1 - d],
                u_ss.at[sweep, d], u_rs.at[sweep, others - 1 - d], (sector_of(d + 1), t),
            ).wait_send()

    @pl.loop(1, n_slab)
    def _(k):
        b_copy(k, t).wait_send()


def body(n_sector, n_slab, *args):
    vmem = pl.BlockSpec(memory_space=pltpu.VMEM)
    smem = pl.BlockSpec(memory_space=pltpu.SMEM)
    others = n_sector - 1
    rounds = SWEEPS - 1
    block = (LAYERS, ROWS, COLS)
    tiles = (CHUNKS, 128)

    def f32(*shape):
        return pltpu.VMEM(shape, F32)

    def i32(*shape):
        return pltpu.VMEM(shape, jnp.int32)

    def sem(*shape):
        return pltpu.SemaphoreType.DMA(shape)

    scratch = dict(
        oh=pltpu.VMEM((others, CELLS_HI, SLOTS), BF),
        ohlo=pltpu.VMEM((others, 128, SLOTS), BF),
        fsplit=pltpu.VMEM((3, 384, CELLS_HI), BF),
        acc=f32(4, 384, CELLS_HI),
        cell=i32(others, *tiles),
        fweight=f32(others, *tiles),
        fup=i32(others, *tiles),
        own=f32(others, 4, *tiles),
        far=f32(others, 4, *tiles),
        link=f32(others, *tiles),
        vals=f32(others, 4, *tiles),
        up_stage=f32(5, ROWS, COLS),
        dn_stage=f32(3, ROWS, COLS),
        halo_lo=f32(5, ROWS, COLS),
        halo_hi=f32(3, ROWS, COLS),
        rup_stage=f32(5, LAYERS, COLS),
        rdn_stage=f32(3, LAYERS, COLS),
        rhalo_lo=f32(5, LAYERS, COLS),
        rhalo_hi=f32(3, LAYERS, COLS),
        asend=f32(16, 128),
        arecv=f32(others, 16, 128),
        bsend=f32(4, 128),
        brecv=f32(n_slab, 4, 128),
        cz=f32(LAYERS + 1, ROWS, COLS),
        cxu=f32(*block),
        cxd=f32(*block),
        cyu=f32(*block),
        cyd=f32(*block),
        storage=f32(*block),
        rhs=f32(*block),
        inv=f32(*block),
        ubuf=f32(*block),
        part=f32(*block),
        uown=f32(rounds, others, *tiles),
        urecv=f32(rounds, others, *tiles),
        usend=f32(rounds, 2, ROWS, COLS),
        zlo=f32(rounds, ROWS, COLS),
        zhi=f32(rounds, ROWS, COLS),
        xup=f32(rounds, LAYERS, COLS),
        xdn=f32(rounds, LAYERS, COLS),
        xlo=f32(rounds, LAYERS, COLS),
        xhi=f32(rounds, LAYERS, COLS),
        f_ss=sem(others), f_rs=sem(others),
        h_ss=sem(4), h_rs=sem(4),
        a_ss=sem(others), a_rs=sem(others),
        b_ss=sem(n_slab - 1), b_rs=sem(n_slab - 1),
        u_ss=sem(rounds, others), u_rs=sem(rounds, others),
        w_ss=sem(rounds, 4), w_rs=sem(rounds, 4),
    )
    names = list(scratch)

    def run(*refs):
        kernel(n_sector, n_slab, *refs[:12], **dict(zip(names, refs[12:])))

    in_specs = [vmem] * 10
    in_specs[7] = smem
    return pl.pallas_call(
        run,
        out_shape=(
            jax.ShapeDtypeStruct((3, *block), F32),
            jax.ShapeDtypeStruct(block, F32),
        ),
        in_specs=in_specs,
        out_specs=(vmem, vmem),
        scratch_shapes=list(scratch.values()),
        compiler_params=pltpu.CompilerParams(
            collective_id=0, has_side_effects=True, vmem_limit_bytes=48 * 2**20
        ),
    )(*args)


def solution(mesh):
    placed = (
        P("slab", "sector", None),
        P(None, "slab", "sector", None),
        P(None, "slab", "sector", None),
        P("slab", "sector", None),
        P(None, "slab", "sector", None),
        P("slab", "sector", None),
        P("slab", "sector", None, None),
        P("slab", "sector", None),
        P("slab", "sector", None, None),
        P("slab", "sector", None, None),
    )
    return jax.shard_map(
        functools.partial(body, mesh.shape["sector"], mesh.shape["slab"]),
        mesh=mesh,
        in_specs=placed,
        out_specs=(P(None, "slab", "sector", None), P("slab", "sector", None)),
        check_vma=False,
    )
```

time: 1480 us -> 73 us (0.05); the launches traced: 1460 us -> 72.5 us
  local copies, waits for them, and re-layouts: 445 us -> 9.97 us
  loops' own time: 420 us -> 0 us
  other arithmetic: 311 us -> 0 us
  between operations: 141 us -> 0.66 us
  starting transfers between devices: 91 us -> 0 us
  Pallas kernels: 0 us -> 61.9 us
  blocking collectives: 51.3 us -> 0 us
    another operation x2 -> x0, loops' own time: 420 us -> none  [coarse_solve(): lax.linalg.tridiagonal_solve(-below, diagonal, upper, source[:, None])[:, 0]]
    gather x5 -> x0, local copies, waits for them, and re-layouts: 356 us -> none  [the longest x4 322 us: body(): update.reshape(-1)[flat_index].reshape(sector_count, slot_count)]
    scatter-add x6 -> x0, other arithmetic: 269 us -> none  [the longest x4 173 us: body(): extra = jnp.zeros((layer_count * row_count * column_count,), jnp.float32)...]
    pallas_call x0 -> x1, Pallas kernels: none -> 61.9 us  [body(): pl.pallas_call(run, out_shape=(jax.ShapeDtypeStruct((3, *block), F32), ja...]
    ppermute x20 -> x0, starting transfers between devices: 53.5 us -> none  [the longest x10 37.3 us: padded_2(): lax.ppermute(tail, axis, [(i, (i + 1) % count) for i in range(ends)])]
    slice x64 -> x0, local copies, waits for them, and re-layouts: 47.7 us -> none  [the longest x54 34.7 us: coarse_solve(): lax.linalg.tridiagonal_solve(-below, diagonal, upper, source[:, None])[:, 0]]
    all_gather x1 -> x0, blocking collectives: 40.8 us -> none  [body(): coarse_rows = lax.all_gather(summed, 'slab', axis=1, tiled=True)]
    all_to_all x5 -> x0, starting transfers between devices: 37.6 us -> none  [the longest x4 32.3 us: body(): lax.all_to_all(own_update, 'sector', split_axis=0, concat_axis=0, tiled=T...]
  transfers between devices with their start and end apart: 25 -> 0, of which waited for: 1 -> 0; matrix products, arithmetic and copies ran while one was open for 42% -> 0% of each run, Pallas kernels for 0% -> 0%
where the time goes in v1:
time: 73 us; the launch traced here: 72.5 us
  Pallas kernels  61.9 us (85%)
  local copies, waits for them, and re-layouts  9.97 us (14%)
    pallas_call x1, Pallas kernels, body(): pl.pallas_call(run, out_shape=(jax.ShapeDtypeStruct((3, *block), F32), ja...  61.9 us
    unnamed x22, local copies, waits for them, and re-layouts  9.97 us

profile of v1, /device:TPU:1, one launch (start us, length us, event | category | flops | bytes accessed | tf_op | source)
XLA Modules:
  0.0 72.5 jit_solution(12126252207118031227)
XLA Ops:
  0.6 0.0 copy-start
  0.6 1.0 %copy-done = f32[3,4,64,128]{3,2,1,0:T(8,128)S(1)} copy-done((f32[3,4,64,128]{3,2,1,0:T(8,128)S(1)}, f32[3,4,64,128]{3,2,1,0:T(8,128)}, u32[]{:S(2)}) %copy-start) | copy-done | bytes 393240
  1.6 0.0 copy-start.1
  1.6 1.0 %copy-done.1 = f32[3,4,64,128]{3,2,1,0:T(8,128)S(1)} copy-done((f32[3,4,64,128]{3,2,1,0:T(8,128)S(1)}, f32[3,4,64,128]{3,2,1,0:T(8,128)}, u32[]{:S(2)}) %copy-start.1) | copy-done | bytes 393240
  2.6 0.0 copy-start.2
  2.6 0.9 %copy-done.2 = f32[2,4,64,128]{3,2,1,0:T(8,128)S(1)} copy-done((f32[2,4,64,128]{3,2,1,0:T(8,128)S(1)}, f32[2,4,64,128]{3,2,1,0:T(8,128)}, u32[]{:S(2)}) %copy-start.2) | copy-done | bytes 262168
  3.6 0.0 copy-start.3
  3.6 0.9 %copy-done.3 = f32[4,64,128]{2,1,0:T(8,128)S(1)} copy-done((f32[4,64,128]{2,1,0:T(8,128)S(1)}, f32[4,64,128]{2,1,0:T(8,128)}, u32[]{:S(2)}) %copy-start.3) | copy-done | bytes 131096
  4.5 0.0 copy-start.4
  4.5 0.9 %copy-done.4 = f32[4,64,128]{2,1,0:T(8,128)S(1)} copy-done((f32[4,64,128]{2,1,0:T(8,128)S(1)}, f32[4,64,128]{2,1,0:T(8,128)}, u32[]{:S(2)}) %copy-start.4) | copy-done | bytes 131096
  5.4 0.0 copy-start.5
  5.4 0.9 %copy-done.5 = s32[4,64,128]{2,1,0:T(8,128)S(1)} copy-done((s32[4,64,128]{2,1,0:T(8,128)S(1)}, s32[4,64,128]{2,1,0:T(8,128)}, u32[]{:S(2)}) %copy-start.5) | copy-done | bytes 131096
  6.3 0.0 copy-start.6
  6.3 0.8 %copy-done.6 = s32[1,1,8,1024]{3,2,1,0:T(8,128)S(1)} copy-done((s32[1,1,8,1024]{3,2,1,0:T(8,128)S(1)}, s32[1,1,8,1024]{3,2,1,0:T(8,128)}, u32[]{:S(2)}) %copy-start.6) | copy-done | bytes 32792
  7.0 0.0 copy-start.7
  7.1 0.8 %copy-done.7 = f32[1,1,8,1024]{3,2,1,0:T(8,128)S(1)} copy-done((f32[1,1,8,1024]{3,2,1,0:T(8,128)S(1)}, f32[1,1,8,1024]{3,2,1,0:T(8,128)}, u32[]{:S(2)}) %copy-start.7) | copy-done | bytes 32792
  7.8 0.0 copy-start.8
  7.8 0.8 %copy-done.8 = s32[1,1,8,1024]{3,2,1,0:T(8,128)S(1)} copy-done((s32[1,1,8,1024]{3,2,1,0:T(8,128)S(1)}, s32[1,1,8,1024]{3,2,1,0:T(8,128)}, u32[]{:S(2)}) %copy-start.8) | copy-done | bytes 32792
  8.6 0.0 copy-start.9
  8.6 0.7 copy-done.9
  9.2 61.9 %shard_map.113 = (f32[3,4,64,128]{3,2,1,0:T(8,128)S(1)}, f32[4,64,128]{2,1,0:T(8,128)S(1)}) custom-call(f32[4,64,128]{2,1,0:T(8,128)S(1)} %copy-done.3, f32[2,4,64,128]{3,2,1,0:T(8,128)S(1)} %copy-done.2, f32[3,4,64,128]{3,2,1,0:T(8,128)S(1)} %copy-done, f32[4,64,128]{2,1,0:T(8,128)S(1)} %copy-done.4, f32[3,4,64,128]{3,2,1,0:T(8,128)S(1)} %copy-done.1, ...), custom_call_target="tpu_custom_call" | custom-call | tf_op jit(solution)/shard_map/pallas_call | solution.py:561
  71.1 0.7 %copy.14 = f32[3,4,64,128]{3,2,1,0:T(8,128)} copy(f32[3,4,64,128]{3,2,1,0:T(8,128)S(1)} %get-tuple-element.4) | data formatting | bytes 786432
  71.8 0.7 copy.15
Async XLA Ops:
  0.6 1.0 %copy-start = (f32[3,4,64,128]{3,2,1,0:T(8,128)S(1)}, f32[3,4,64,128]{3,2,1,0:T(8,128)}, u32[]{:S(2)}) copy-start(f32[3,4,64,128]{3,2,1,0:T(8,128)} %refs_2_.1) | copy-start | bytes 1179652
  1.6 1.0 %copy-start.1 = (f32[3,4,64,128]{3,2,1,0:T(8,128)S(1)}, f32[3,4,64,128]{3,2,1,0:T(8,128)}, u32[]{:S(2)}) copy-start(f32[3,4,64,128]{3,2,1,0:T(8,128)} %refs_4_.1) | copy-start | bytes 1179652
  2.6 0.9 %copy-start.2 = (f32[2,4,64,128]{3,2,1,0:T(8,128)S(1)}, f32[2,4,64,128]{3,2,1,0:T(8,128)}, u32[]{:S(2)}) copy-start(f32[2,4,64,128]{3,2,1,0:T(8,128)} %refs_1_.1) | copy-start | bytes 786436
  3.6 0.9 %copy-start.3 = (f32[4,64,128]{2,1,0:T(8,128)S(1)}, f32[4,64,128]{2,1,0:T(8,128)}, u32[]{:S(2)}) copy-start(f32[4,64,128]{2,1,0:T(8,128)} %refs_0_.1) | copy-start | bytes 393220
  4.5 0.9 %copy-start.4 = (f32[4,64,128]{2,1,0:T(8,128)S(1)}, f32[4,64,128]{2,1,0:T(8,128)}, u32[]{:S(2)}) copy-start(f32[4,64,128]{2,1,0:T(8,128)} %refs_3_.1) | copy-start | bytes 393220
  5.4 0.9 %copy-start.5 = (s32[4,64,128]{2,1,0:T(8,128)S(1)}, s32[4,64,128]{2,1,0:T(8,128)}, u32[]{:S(2)}) copy-start(s32[4,64,128]{2,1,0:T(8,128)} %refs_5_.1) | copy-start | bytes 393220
  6.3 0.8 %copy-start.6 = (s32[1,1,8,1024]{3,2,1,0:T(8,128)S(1)}, s32[1,1,8,1024]{3,2,1,0:T(8,128)}, u32[]{:S(2)}) copy-start(s32[1,1,8,1024]{3,2,1,0:T(8,128)} %refs_6_.1) | copy-start | bytes 98308
  7.0 0.8 %copy-start.7 = (f32[1,1,8,1024]{3,2,1,0:T(8,128)S(1)}, f32[1,1,8,1024]{3,2,1,0:T(8,128)}, u32[]{:S(2)}) copy-start(f32[1,1,8,1024]{3,2,1,0:T(8,128)} %refs_8_.1) | copy-start | bytes 98308
  7.8 0.8 %copy-start.8 = (s32[1,1,8,1024]{3,2,1,0:T(8,128)S(1)}, s32[1,1,8,1024]{3,2,1,0:T(8,128)}, u32[]{:S(2)}) copy-start(s32[1,1,8,1024]{3,2,1,0:T(8,128)} %refs_9_.1) | copy-start | bytes 98308
  8.6 0.7 copy-start.9

commit v2 on v1

--- a/solution.py
+++ b/solution.py
@@ -50,9 +50,9 @@
 
 def kernel(
     n_sector, n_slab,
-    p_ref, s_ref, om_ref, pv_ref, tr_ref, bits_ref, fc_ref, cnt_ref, ft_ref, fu_ref,
-    res_ref, out_ref, *,
-    oh, ohlo, fsplit, acc, cell, fweight, fup, own, far, link, vals,
+    inputs, res_ref, out_ref, *,
+    p_ref, s_ref, om_ref, pv_ref, tr_ref, bits_ref, fc_ref, cnt_ref, ft_ref, fu_ref, in_sem,
+    oh, ohlo, fsplit, cell, fweight, fup, own, far, link, vals,
     up_stage, dn_stage, halo_lo, halo_hi, rup_stage, rdn_stage, rhalo_lo, rhalo_hi,
     asend, arecv, bsend, brecv,
     cz, cxu, cxd, cyu, cyd, storage, rhs, inv, ubuf, part,
@@ -73,9 +73,19 @@
             device_id=device, device_id_type=MESH,
         )
 
+    far_first = sorted(range(others), key=lambda d: (-min(d + 1, n_sector - d - 1), d))
+    arrivals = [others - 1 - d for d in far_first]
+
     def sector_of(d):
         return lax.rem(me + d, n_sector)
 
+    held = (p_ref, s_ref, om_ref, pv_ref, tr_ref, bits_ref, fc_ref, cnt_ref, ft_ref, fu_ref)
+    loads = [
+        pltpu.make_async_copy(src, dst, in_sem.at[i])
+        for i, (src, dst) in enumerate(zip(inputs, held))
+    ]
+    for i in (6, 7, 8, 9, 0, 1, 4, 5, 3, 2):
+        loads[i].start()
     barrier = pltpu.get_barrier_semaphore()
 
     @pl.loop(1, n_sector)
@@ -88,6 +98,8 @@
             barrier, inc=1, device_id=(me, lax.rem(t + k, n_slab)), device_id_type=MESH
         )
 
+    for i in (6, 7, 8, 9, 0, 1, 4, 5):
+        loads[i].wait()
     top = LAYERS - 1
     for i, plane in enumerate((p_ref[top], s_ref[0, top], s_ref[1, top], tr_ref[0, top])):
         up_stage[i] = plane
@@ -146,26 +158,28 @@
         c.start()
 
     def gather(d, weights, count, store):
-        for b in range(CHUNKS // 2):
-            picks = oh[d, :, b * 256 : (b + 1) * 256]
-            rows = [jnp.bitwise_and(cell[d, 2 * b + k : 2 * b + k + 1, :], 127) for k in range(2)]
-            for i, w in enumerate(weights):
+        rows = [jnp.bitwise_and(cell[d, b : b + 1, :], 127) for b in range(CHUNKS)]
+        for i, w in enumerate(weights):
+            for b in range(CHUNKS // 2):
+                picks = oh[d, :, b * 256 : (b + 1) * 256]
                 g = jnp.dot(w, picks, preferred_element_type=F32)
                 total = g[(count - 1) * 128 :]
                 for j in reversed(range(count - 1)):
                     total = g[j * 128 : (j + 1) * 128] + total
                 for k in range(2):
-                    found = jnp.where(sub == rows[k], total[:, k * 128 : (k + 1) * 128], 0.0)
+                    found = jnp.where(
+                        sub == rows[2 * b + k], total[:, k * 128 : (k + 1) * 128], 0.0
+                    )
                     store(i, 2 * b + k, jnp.sum(found, axis=0, keepdims=True))
 
     def fault_copy(d):
         return copy(own.at[d], far.at[others - 1 - d], f_ss.at[d], f_rs.at[others - 1 - d],
                     (sector_of(d + 1), t))
 
-    @pl.loop(0, others)
-    def _(d):
-        def store(i, b, row):
-            own[d, i, pl.ds(b, 1), :] = row
+    for d in far_first:
+
+        def store(i, b, row, d=d):
+            own[d, i, b : b + 1, :] = row
 
         gather(d, [fsplit[i] for i in range(3)], 3, store)
         own[d, 3] = jnp.right_shift(cell[d], 13).astype(F32)
@@ -178,6 +192,8 @@
     not_first_sector = jnp.where(me > 0, 1.0, 0.0).astype(F32)
     not_last_sector = jnp.where(me < n_sector - 1, 1.0, 0.0).astype(F32)
 
+    loads[3].wait()
+    loads[2].wait()
     for k in range(LAYERS):
         p = p_ref[k]
         pv = pv_ref[k]
@@ -266,7 +282,7 @@
 
     zero_tile = jnp.zeros((CHUNKS, 128), F32)
     layer_source = [zero_tile] * LAYERS
-    for d in range(others):
+    for d in arrivals:
         fault_copy(others - 1 - d).wait_recv()
         flags = fup[d]
         w = fweight[d]
@@ -301,35 +317,31 @@
     def _(d):
         a_copy(d).start()
 
-    def masked(d, field, count):
+    nt = (((1,), (1,)), ((), ()))
+
+    def masked(d, field):
         pieces = []
         for b in range(CHUNKS):
-            value = field[b : b + 1, :]
             mask = ohlo[d, :, b * 128 : (b + 1) * 128]
-            pieces.append(jnp.concatenate([mask * x for x in split(value, count)], 0))
+            parts = split(field[b : b + 1, :], 2)
+            pieces.append(jnp.concatenate([mask * x for x in parts], 0))
         return jnp.concatenate(pieces, 1)
 
-    nt = (((1,), (1,)), ((), ()))
-    acc[...] = jnp.zeros(acc.shape, F32)
-
-    @pl.loop(0, others)
-    def _(d):
-        for i in range(4):
-            acc[i] += lax.dot_general(
-                masked(d, vals.at[d, i], 3), oh[d], nt, preferred_element_type=F32
-            )
-
-    def unfold(total):
-        return total.T.reshape(LAYERS, ROWS, COLS)
-
-    for i in range(4):
-        placed = unfold(acc[i, :128] + (acc[i, 128:256] + acc[i, 256:]))
-        if i < 3:
-            res_ref[i] += placed
-        else:
-            inv[...] = RELAXATION / (inv[...] + placed)
-    for k in range(LAYERS):
-        rhs[k] = -(res_ref[0, k] + res_ref[1, k] + res_ref[2, k])
+    def scatter(fields):
+        total = None
+        for d in range(others):
+            rows = jnp.concatenate([masked(d, vals.at[d, i]) for i in fields], 0)
+            part = lax.dot_general(rows, oh[d], nt, preferred_element_type=F32)
+            total = part if total is None else total + part
+        return [
+            (total[256 * i : 256 * i + 128] + total[256 * i + 128 : 256 * i + 256])
+            .T.reshape(LAYERS, ROWS, COLS)
+            for i in range(len(fields))
+        ]
+
+    placed = scatter((0, 1))
+    res_ref[0] += placed[0]
+    res_ref[1] += placed[1]
 
     sums = asend[...]
     for d in range(others):
@@ -339,7 +351,8 @@
     lane16 = lax.broadcasted_iota(jnp.int32, (16, 128), 1)
     row16 = lax.broadcasted_iota(jnp.int32, (16, 128), 0)
     spread = jnp.where(
-        jnp.bitwise_and(lane16, 3) == jnp.bitwise_and(row16, 3), jnp.broadcast_to(column, (16, 128)), 0.0
+        jnp.bitwise_and(lane16, 3) == jnp.bitwise_and(row16, 3),
+        jnp.broadcast_to(column, (16, 128)), 0.0,
     )
     for q in range(4):
         bsend[q : q + 1, :] = jnp.sum(spread[4 * q : 4 * q + 4], axis=0, keepdims=True)
@@ -352,6 +365,12 @@
     @pl.loop(1, n_slab)
     def _(k):
         b_copy(k, t).start()
+
+    placed = scatter((2, 3))
+    res_ref[2] += placed[0]
+    inv[...] = RELAXATION / (inv[...] + placed[1])
+    for k in range(LAYERS):
+        rhs[k] = -(res_ref[0, k] + res_ref[1, k] + res_ref[2, k])
 
     @pl.loop(1, n_slab)
     def _(k):
@@ -387,15 +406,15 @@
     def level_row(k):
         return level[k + 1 : k + 2]
 
-    def fault_extra(value_of):
-        def body(d, total):
+    def fault_extra(order, value_of):
+        total = None
+        for d in order:
             vals[d, 0] = link[d] * value_of(d)
-            return total + lax.dot_general(
-                masked(d, vals.at[d, 0], 2), oh[d], nt, preferred_element_type=F32
+            part = lax.dot_general(
+                oh[d], masked(d, vals.at[d, 0]), nt, preferred_element_type=F32
             )
-
-        total = lax.fori_loop(0, others, body, jnp.zeros((256, 256), F32))
-        return unfold(total[:128] + total[128:])
+            total = part if total is None else total + part
+        return (total[:, :128] + total[:, 128:]).reshape(LAYERS, ROWS, COLS)
 
     def coarse_far(d):
         value = zero_tile
@@ -403,7 +422,7 @@
             value = jnp.where(far[d, 3] == k, level_row(k), value)
         return value
 
-    part[...] = fault_extra(coarse_far)
+    part[...] = fault_extra(range(others), coarse_far)
     for k in range(LAYERS):
         here = level_row(k)
         total = part[k] + rhs[k] + cz[k + 1] * level_row(k + 1) + cz[k] * level_row(k - 1)
@@ -436,12 +455,13 @@
                 u_ss.at[sweep, d], u_rs.at[sweep, others - 1 - d], (sector_of(d + 1), t),
             )
 
-        @pl.loop(0, others)
-        def _(d, sweep=sweep, u_copy=u_copy):
-            def store(i, b, row):
-                uown[sweep, d, pl.ds(b, 1), :] = row
-
-            gather(d, [fsplit[0, :256]], 2, store)
+        weights = fsplit[0, :256]
+        for d in far_first:
+
+            def store(i, b, row, d=d):
+                uown[sweep, d, b : b + 1, :] = row
+
+            gather(d, [weights], 2, store)
             u_copy(d).start()
 
         for k in range(LAYERS):
@@ -454,6 +474,12 @@
             if k < top:
                 total = total + cz[k + 1] * ubuf[k + 1]
             part[k] = total
+
+        def arrived(d, sweep=sweep, u_copy=u_copy):
+            u_copy(others - 1 - d).wait_recv()
+            return urecv[sweep, d]
+
+        extra = fault_extra(arrivals, arrived)
         for c in edge_copies:
             c.wait_recv()
         part[0] += cz[0] * zlo[sweep]
@@ -461,10 +487,7 @@
         for k in range(LAYERS):
             part[k, last:] += cxu[k, last:] * xhi[sweep, k : k + 1, :]
             part[k, :1] += cxd[k, :1] * xlo[sweep, k : k + 1, :]
-        for d in range(others):
-            u_copy(others - 1 - d).wait_recv()
         target = out_ref if sweep == SWEEPS - 2 else ubuf
-        extra = fault_extra(lambda d, sweep=sweep: urecv[sweep, d])
         for k in range(LAYERS):
             target[k] = (1.0 - RELAXATION) * ubuf[k] + inv[k] * (part[k] + extra[k])
 
@@ -486,7 +509,6 @@
 
 def body(n_sector, n_slab, *args):
     vmem = pl.BlockSpec(memory_space=pltpu.VMEM)
-    smem = pl.BlockSpec(memory_space=pltpu.SMEM)
     others = n_sector - 1
     rounds = SWEEPS - 1
     block = (LAYERS, ROWS, COLS)
@@ -502,10 +524,20 @@
         return pltpu.SemaphoreType.DMA(shape)
 
     scratch = dict(
+        p_ref=f32(*block),
+        s_ref=f32(2, *block),
+        om_ref=f32(3, *block),
+        pv_ref=f32(*block),
+        tr_ref=f32(3, *block),
+        bits_ref=i32(*block),
+        fc_ref=i32(1, 1, n_sector, SLOTS),
+        cnt_ref=pltpu.SMEM((1, 1, n_sector), jnp.int32),
+        ft_ref=f32(1, 1, n_sector, SLOTS),
+        fu_ref=i32(1, 1, n_sector, SLOTS),
+        in_sem=sem(10),
         oh=pltpu.VMEM((others, CELLS_HI, SLOTS), BF),
         ohlo=pltpu.VMEM((others, 128, SLOTS), BF),
         fsplit=pltpu.VMEM((3, 384, CELLS_HI), BF),
-        acc=f32(4, 384, CELLS_HI),
         cell=i32(others, *tiles),
         fweight=f32(others, *tiles),
         fup=i32(others, *tiles),
@@ -554,21 +586,19 @@
     names = list(scratch)
 
     def run(*refs):
-        kernel(n_sector, n_slab, *refs[:12], **dict(zip(names, refs[12:])))
-
-    in_specs = [vmem] * 10
-    in_specs[7] = smem
+        kernel(n_sector, n_slab, refs[:10], *refs[10:12], **dict(zip(names, refs[12:])))
+
     return pl.pallas_call(
         run,
         out_shape=(
             jax.ShapeDtypeStruct((3, *block), F32),
             jax.ShapeDtypeStruct(block, F32),
         ),
-        in_specs=in_specs,
+        in_specs=[pl.BlockSpec(memory_space=pltpu.HBM)] * 10,
         out_specs=(vmem, vmem),
         scratch_shapes=list(scratch.values()),
         compiler_params=pltpu.CompilerParams(
-            collective_id=0, has_side_effects=True, vmem_limit_bytes=48 * 2**20
+            collective_id=0, has_side_effects=True, vmem_limit_bytes=60 * 2**20
         ),
     )(*args)
 

time: 73 us -> 57.2 us (0.78)
  Pallas kernels: 61.9 us -> 53.9 us
  local copies, waits for them, and re-layouts: 9.97 us -> 2.46 us
    pallas_call x1, Pallas kernels: 61.9 us -> 53.9 us  [body(): pl.pallas_call(run, out_shape=(jax.ShapeDtypeStruct((3, *block), F32), ja...]
    unnamed x22 -> x4, local copies, waits for them, and re-layouts: 9.97 us -> 2.46 us
where the time goes in v2:
time: 57.2 us; the launch traced here: 57 us
  Pallas kernels  53.9 us (94%)
  local copies, waits for them, and re-layouts  2.46 us (4%)
  between operations  0.65 us (1%)
    pallas_call x1, Pallas kernels, body(): pl.pallas_call(run, out_shape=(jax.ShapeDtypeStruct((3, *block), F32), ja...  53.9 us
    unnamed x4, local copies, waits for them, and re-layouts  2.46 us

profile of v2, /device:TPU:1, one launch (start us, length us, event | category | flops | bytes accessed | tf_op | source)
XLA Modules:
  0.0 57.0 jit_solution(12208599230085884904)
XLA Ops:
  0.6 53.9 %shard_map.113 = (f32[3,4,64,128]{3,2,1,0:T(8,128)}, f32[4,64,128]{2,1,0:T(8,128)}) custom-call(f32[4,64,128]{2,1,0:T(8,128)} %refs_0_.1, f32[2,4,64,128]{3,2,1,0:T(8,128)} %refs_1_.1, f32[3,4,64,128]{3,2,1,0:T(8,128)} %refs_2_.1, f32[4,64,128]{2,1,0:T(8,128)} %refs_3_.1, f32[3,4,64,128]{3,2,1,0:T(8,128)} %refs_4_.1, s32[4,64,128]{2,1,0:T(8,128)} %refs_5_.1, ...), custom_call_target="tpu_custom_call" | custom-call | tf_op jit(solution)/shard_map/pallas_call | solution.py:591
  54.6 0.0 copy-start
  54.6 1.8 %copy.14 = f32[3,4,64,128]{3,2,1,0:T(8,128)} copy(f32[3,4,64,128]{3,2,1,0:T(8,128)} %get-tuple-element.4) | data formatting | bytes 786432
  56.4 0.0 copy-done
  56.4 0.7 %copy.15 = f32[4,64,128]{2,1,0:T(8,128)} copy(f32[4,64,128]{2,1,0:T(8,128)S(1)} %copy-done) | data formatting | bytes 262144
Async XLA Ops:
  54.6 1.8 %copy-start = (f32[4,64,128]{2,1,0:T(8,128)S(1)}, f32[4,64,128]{2,1,0:T(8,128)}, u32[]{:S(2)}) copy-start(f32[4,64,128]{2,1,0:T(8,128)} %get-tuple-element.5) | copy-start | bytes 393220

commit v3 on v2

--- a/solution.py
+++ b/solution.py
@@ -55,8 +55,8 @@
     oh, ohlo, fsplit, cell, fweight, fup, own, far, link, vals,
     up_stage, dn_stage, halo_lo, halo_hi, rup_stage, rdn_stage, rhalo_lo, rhalo_hi,
     asend, arecv, bsend, brecv,
-    cz, cxu, cxd, cyu, cyd, storage, rhs, inv, ubuf, part,
-    uown, urecv, usend, zlo, zhi, xup, xdn, xlo, xhi,
+    cz, cxu, cxd, cyu, cyd, storage, rhs, inv, ubufs, part, to_layer,
+    uown, urecv, zlo, zhi, xup, xdn, xlo, xhi,
     f_ss, f_rs, h_ss, h_rs, a_ss, a_rs, b_ss, b_rs, u_ss, u_rs, w_ss, w_rs,
 ):
     me = lax.axis_index("sector")
@@ -73,11 +73,15 @@
             device_id=device, device_id_type=MESH,
         )
 
-    far_first = sorted(range(others), key=lambda d: (-min(d + 1, n_sector - d - 1), d))
-    arrivals = [others - 1 - d for d in far_first]
-
-    def sector_of(d):
-        return lax.rem(me + d, n_sector)
+    chips = n_sector // 2
+    reach = sorted(range(1, chips), key=lambda c: (-min(c, chips - c), c))
+    partners = [(c, other) for c in reach for other in (0, 1)] + [(0, 1)]
+    mirror = [partners.index(((chips - c) % chips, other)) for c, other in partners]
+    chip, core = me // 2, lax.rem(me, 2)
+
+    def sector_of(i):
+        c, other = partners[i]
+        return lax.rem(chip + c, chips) * 2 + (1 - core if other else core)
 
     held = (p_ref, s_ref, om_ref, pv_ref, tr_ref, bits_ref, fc_ref, cnt_ref, ft_ref, fu_ref)
     loads = [
@@ -88,9 +92,8 @@
         loads[i].start()
     barrier = pltpu.get_barrier_semaphore()
 
-    @pl.loop(1, n_sector)
-    def _(d):
-        pl.semaphore_signal(barrier, inc=1, device_id=(sector_of(d), t), device_id_type=MESH)
+    for i in range(others):
+        pl.semaphore_signal(barrier, inc=1, device_id=(sector_of(i), t), device_id_type=MESH)
 
     @pl.loop(1, n_slab)
     def _(k):
@@ -101,9 +104,6 @@
     for i in (6, 7, 8, 9, 0, 1, 4, 5):
         loads[i].wait()
     top = LAYERS - 1
-    for i, plane in enumerate((p_ref[top], s_ref[0, top], s_ref[1, top], tr_ref[0, top])):
-        up_stage[i] = plane
-    up_stage[4] = bits_ref[top].astype(F32)
     for i, plane in enumerate((p_ref[0], s_ref[0, 0], s_ref[1, 0])):
         dn_stage[i] = plane
     last = ROWS - 1
@@ -117,18 +117,23 @@
             rdn_stage[i, k : k + 1, :] = row
 
     lane = lax.broadcasted_iota(jnp.int32, (1, 128), 1)
-    counts = [cnt_ref[0, 0, sector_of(d)] for d in range(1, n_sector)]
-    turn = lax.rem(n_sector - me, n_sector)
+    counts = [cnt_ref[0, 0, sector_of(d)] for d in range(others)]
+    turn = lax.rem(n_sector - 2 * chip, n_sector)
+    first_core = core == 0
     for b in range(CHUNKS):
         span = slice(b * 128, (b + 1) * 128)
         cells = pltpu.roll(fc_ref[0, 0, :, span], turn, 0)
         flags = pltpu.roll(fu_ref[0, 0, :, span], turn, 0)
         trans = pltpu.roll(ft_ref[0, 0, :, span], turn, 0)
-        for d in range(others):
-            row = slice(d + 1, d + 2)
-            cell[d, b : b + 1, :] = cells[row]
-            fup[d, b : b + 1, :] = flags[row]
-            fweight[d, b : b + 1, :] = jnp.where(lane + b * 128 < counts[d], trans[row], 0.0)
+        for d, (c, other) in enumerate(partners):
+            here, there = 2 * c + other, 2 * c + 1 - other
+
+            def pick(x):
+                return jnp.where(first_core, x[here : here + 1], x[there : there + 1])
+
+            cell[d, b : b + 1, :] = pick(cells)
+            fup[d, b : b + 1, :] = pick(flags)
+            fweight[d, b : b + 1, :] = jnp.where(lane + b * 128 < counts[d], pick(trans), 0.0)
 
     for i, field in enumerate((p_ref, s_ref.at[0], s_ref.at[1])):
         flipped = field[...].reshape(CELLS_HI, COLS).T
@@ -145,17 +150,6 @@
             c = cell[d, b : b + 1, :]
             oh[d, :, span] = jnp.where(sub_hi == jnp.right_shift(c, 7), 1.0, 0.0).astype(BF)
             ohlo[d, :, span] = jnp.where(sub == jnp.bitwise_and(c, 127), 1.0, 0.0).astype(BF)
-
-    pl.semaphore_wait(barrier, n_sector - 1 + n_slab - 1)
-
-    halo_copies = [
-        copy(up_stage, halo_lo, h_ss.at[0], h_rs.at[0], (me, t_next)),
-        copy(dn_stage, halo_hi, h_ss.at[1], h_rs.at[1], (me, t_prev)),
-        copy(rup_stage, rhalo_lo, h_ss.at[2], h_rs.at[2], (s_next, t)),
-        copy(rdn_stage, rhalo_hi, h_ss.at[3], h_rs.at[3], (s_prev, t)),
-    ]
-    for c in halo_copies:
-        c.start()
 
     def gather(d, weights, count, store):
         rows = [jnp.bitwise_and(cell[d, b : b + 1, :], 127) for b in range(CHUNKS)]
@@ -173,17 +167,16 @@
                     store(i, 2 * b + k, jnp.sum(found, axis=0, keepdims=True))
 
     def fault_copy(d):
-        return copy(own.at[d], far.at[others - 1 - d], f_ss.at[d], f_rs.at[others - 1 - d],
-                    (sector_of(d + 1), t))
-
-    for d in far_first:
+        return copy(own.at[d], far.at[mirror[d]], f_ss.at[d], f_rs.at[mirror[d]],
+                    (sector_of(d), t))
+
+    for d in range(others):
 
         def store(i, b, row, d=d):
             own[d, i, b : b + 1, :] = row
 
         gather(d, [fsplit[i] for i in range(3)], 3, store)
         own[d, 3] = jnp.right_shift(cell[d], 13).astype(F32)
-        fault_copy(d).start()
 
     lane2 = lax.broadcasted_iota(jnp.int32, (ROWS, COLS), 1)
     row2 = lax.broadcasted_iota(jnp.int32, (ROWS, COLS), 0)
@@ -228,19 +221,66 @@
                 res_ref[a, k] -= flux[a]
                 res_ref[a, k - 1] += flux[a]
 
+    pl.semaphore_wait(barrier, n_sector - 1 + n_slab - 1)
+
+    halo_copies = [
+        copy(dn_stage, halo_hi, h_ss.at[1], h_rs.at[1], (me, t_prev)),
+        copy(rup_stage, rhalo_lo, h_ss.at[2], h_rs.at[2], (s_next, t)),
+        copy(rdn_stage, rhalo_hi, h_ss.at[3], h_rs.at[3], (s_prev, t)),
+    ]
+    for c in halo_copies:
+        c.start()
+    for d in range(others):
+        fault_copy(d).start()
+
+    zero_tile = jnp.zeros((CHUNKS, 128), F32)
+    layer_source = [zero_tile] * LAYERS
+    for d in range(others):
+        fault_copy(d).wait_recv()
+    for d in range(others):
+        flags = fup[d]
+        w = fweight[d]
+        flux, coupling = face(
+            own[d, 0], mobilities(own[d, 1], own[d, 2]), w, flags,
+            far[d, 0], mobilities(far[d, 1], far[d, 2]), 0,
+        )
+        for a in range(3):
+            vals[d, a] = flux[a]
+        vals[d, 3] = coupling
+        link[d] = coupling
+        layer = jnp.right_shift(cell[d], 13)
+        for k in range(LAYERS):
+            layer_source[k] = layer_source[k] - jnp.where(layer == k, flux[2], 0.0)
+
+    nt = (((1,), (1,)), ((), ()))
+
+    def masked(d, field):
+        pieces = []
+        for b in range(CHUNKS):
+            mask = ohlo[d, :, b * 128 : (b + 1) * 128]
+            parts = split(field[b : b + 1, :], 2)
+            pieces.append(jnp.concatenate([mask * x for x in parts], 0))
+        return jnp.concatenate(pieces, 1)
+
+    def scatter(fields):
+        total = None
+        for d in range(others):
+            rows = jnp.concatenate([masked(d, vals.at[d, i]) for i in fields], 0)
+            part = lax.dot_general(rows, oh[d], nt, preferred_element_type=F32)
+            total = part if total is None else total + part
+        return [
+            (total[256 * i : 256 * i + 128] + total[256 * i + 128 : 256 * i + 256])
+            .T.reshape(LAYERS, ROWS, COLS)
+            for i in range(len(fields))
+        ]
+
+    placed = scatter((0, 1))
+    res_ref[0] += placed[0]
+    res_ref[1] += placed[1]
+
     for c in halo_copies:
         c.wait_recv()
 
-    p = p_ref[0]
-    m = mobilities(s_ref[0, 0], s_ref[1, 0])
-    flux, coupling = face(
-        halo_lo[0], mobilities(halo_lo[1], halo_lo[2]), halo_lo[3] * not_first_slab,
-        halo_lo[4].astype(jnp.int32), p, m, 0,
-    )
-    cz[0] = coupling
-    inv[0] += coupling
-    for a in range(3):
-        res_ref[a, 0] -= flux[a]
     p = p_ref[top]
     m = mobilities(s_ref[0, top], s_ref[1, top])
     flux, coupling = face(
@@ -251,6 +291,11 @@
     inv[top] += coupling
     for a in range(3):
         res_ref[a, top] += flux[a]
+        up_stage[a] = flux[a]
+    up_stage[3] = coupling
+    asend[12:13, :] = jnp.sum(flux[0] + flux[1] + flux[2], axis=0, keepdims=True)
+    asend[13:16, :] = jnp.zeros((3, 128), F32)
+    up_copy = copy(up_stage, halo_lo, h_ss.at[0], h_rs.at[0], (me, t_next))
 
     first_p = rdn_stage[0]
     low_flux, low_link = face(
@@ -280,25 +325,6 @@
         for a in range(3):
             res_ref[a, k] += flux[a] - before(flux[a], low_flux[a])
 
-    zero_tile = jnp.zeros((CHUNKS, 128), F32)
-    layer_source = [zero_tile] * LAYERS
-    for d in arrivals:
-        fault_copy(others - 1 - d).wait_recv()
-        flags = fup[d]
-        w = fweight[d]
-        flux, coupling = face(
-            own[d, 0], mobilities(own[d, 1], own[d, 2]), w, flags,
-            far[d, 0], mobilities(far[d, 1], far[d, 2]), 0,
-        )
-        for a in range(3):
-            vals[d, a] = flux[a]
-        vals[d, 3] = coupling
-        link[d] = coupling
-        layer = jnp.right_shift(cell[d], 13)
-        total = flux[0] + flux[1] + flux[2]
-        for k in range(LAYERS):
-            layer_source[k] = layer_source[k] - jnp.where(layer == k, total, 0.0)
-
     for k in range(LAYERS):
         regular = -(res_ref[0, k] + res_ref[1, k] + res_ref[2, k])
         source = jnp.sum(regular, axis=0, keepdims=True) + jnp.sum(
@@ -307,45 +333,23 @@
         asend[k : k + 1, :] = jnp.sum(storage[k], axis=0, keepdims=True)
         asend[4 + k : 5 + k, :] = jnp.sum(cz[k + 1], axis=0, keepdims=True)
         asend[8 + k : 9 + k, :] = source
-    asend[12:16, :] = jnp.zeros((4, 128), F32)
 
     def a_copy(d):
-        return copy(asend, arecv.at[others - 1 - d], a_ss.at[d], a_rs.at[others - 1 - d],
-                    (sector_of(d + 1), t))
-
-    @pl.loop(0, others)
-    def _(d):
+        return copy(asend, arecv.at[mirror[d]], a_ss.at[d], a_rs.at[mirror[d]],
+                    (sector_of(d), t))
+
+    for d in range(others):
         a_copy(d).start()
-
-    nt = (((1,), (1,)), ((), ()))
-
-    def masked(d, field):
-        pieces = []
-        for b in range(CHUNKS):
-            mask = ohlo[d, :, b * 128 : (b + 1) * 128]
-            parts = split(field[b : b + 1, :], 2)
-            pieces.append(jnp.concatenate([mask * x for x in parts], 0))
-        return jnp.concatenate(pieces, 1)
-
-    def scatter(fields):
-        total = None
-        for d in range(others):
-            rows = jnp.concatenate([masked(d, vals.at[d, i]) for i in fields], 0)
-            part = lax.dot_general(rows, oh[d], nt, preferred_element_type=F32)
-            total = part if total is None else total + part
-        return [
-            (total[256 * i : 256 * i + 128] + total[256 * i + 128 : 256 * i + 256])
-            .T.reshape(LAYERS, ROWS, COLS)
-            for i in range(len(fields))
-        ]
-
-    placed = scatter((0, 1))
-    res_ref[0] += placed[0]
-    res_ref[1] += placed[1]
+    up_copy.start()
+
+    placed = scatter((2, 3))
+    res_ref[2] += placed[0]
+    inv[...] += placed[1]
 
     sums = asend[...]
     for d in range(others):
-        a_copy(others - 1 - d).wait_recv()
+        a_copy(d).wait_recv()
+    for d in range(others):
         sums = sums + arecv[d]
     column = jnp.sum(sums, axis=1, keepdims=True)
     lane16 = lax.broadcasted_iota(jnp.int32, (16, 128), 1)
@@ -362,13 +366,27 @@
         return copy(bsend, brecv.at[dst], b_ss.at[k - 1], b_rs.at[k - 1],
                     (me, lax.rem(t + k, n_slab)))
 
-    @pl.loop(1, n_slab)
-    def _(k):
+    def hops(k):
+        z, y, across = k % 8, k // 8, n_slab // 8
+        return min(z, 8 - z) + min(y, across - y)
+
+    for k in sorted(range(1, n_slab), key=lambda k: (-hops(k), k)):
         b_copy(k, t).start()
 
-    placed = scatter((2, 3))
-    res_ref[2] += placed[0]
-    inv[...] = RELAXATION / (inv[...] + placed[1])
+    for d in range(others):
+        for j in range(LAYERS):
+            vals[d, j] = jnp.where(far[d, 3] == j, link[d], 0.0)
+    for j in range(0, LAYERS, 2):
+        placed = scatter((j, j + 1))
+        to_layer[j] = placed[0]
+        to_layer[j + 1] = placed[1]
+
+    up_copy.wait_recv()
+    cz[0] = halo_lo[3]
+    inv[0] += halo_lo[3]
+    for a in range(3):
+        res_ref[a, 0] -= halo_lo[a]
+    inv[...] = RELAXATION / inv[...]
     for k in range(LAYERS):
         rhs[k] = -(res_ref[0, k] + res_ref[1, k] + res_ref[2, k])
 
@@ -380,7 +398,8 @@
     rows = jnp.zeros((4, 128), F32)
     for j in range(n_slab):
         rows = rows + jnp.where(jnp.right_shift(lane4, 2) == j, brecv[j], 0.0)
-    s_row, right, rhs_row = rows[0:1], rows[1:2], rows[2:3]
+    s_row, right = rows[0:1], rows[1:2]
+    rhs_row = rows[2:3] + pltpu.roll(rows[3:4], LAYERS, 1)
     lane1 = lax.broadcasted_iota(jnp.int32, (1, 128), 1)
     right = jnp.where(lane1 < LAYERS * n_slab - 1, right, 0.0)
     s_row = jnp.where(lane1 < LAYERS * n_slab, s_row, 1.0)
@@ -406,44 +425,27 @@
     def level_row(k):
         return level[k + 1 : k + 2]
 
-    def fault_extra(order, value_of):
-        total = None
-        for d in order:
-            vals[d, 0] = link[d] * value_of(d)
-            part = lax.dot_general(
-                oh[d], masked(d, vals.at[d, 0]), nt, preferred_element_type=F32
-            )
-            total = part if total is None else total + part
-        return (total[:, :128] + total[:, 128:]).reshape(LAYERS, ROWS, COLS)
-
-    def coarse_far(d):
-        value = zero_tile
-        for k in range(LAYERS):
-            value = jnp.where(far[d, 3] == k, level_row(k), value)
-        return value
-
-    part[...] = fault_extra(range(others), coarse_far)
     for k in range(LAYERS):
         here = level_row(k)
-        total = part[k] + rhs[k] + cz[k + 1] * level_row(k + 1) + cz[k] * level_row(k - 1)
+        total = rhs[k] + cz[k + 1] * level_row(k + 1) + cz[k] * level_row(k - 1)
         total = total + (cxu[k] + cxd[k] + cyu[k] + cyd[k]) * here
-        ubuf[k] = (1.0 - RELAXATION) * here + inv[k] * total
-
+        for j in range(LAYERS):
+            total = total + to_layer[j, k] * level_row(j)
+        ubufs[0, k] = (1.0 - RELAXATION) * here + inv[k] * total
+
+    block_shape = (LAYERS, ROWS, COLS)
+    groups = [list(range(2)), list(range(2, 4)), list(range(4, others))]
     sends = []
     for sweep in range(SWEEPS - 1):
-        for k in range(LAYERS):
-            xup[sweep, k : k + 1, :] = ubuf[k, last:]
-            xdn[sweep, k : k + 1, :] = ubuf[k, :1]
-        usend[sweep, 0] = ubuf[top]
-        usend[sweep, 1] = ubuf[0]
+        ubuf = ubufs.at[sweep]
         edge_copies = [
-            copy(usend.at[sweep, 0], zlo.at[sweep], w_ss.at[sweep, 0], w_rs.at[sweep, 0], (me, t_next)),
-            copy(usend.at[sweep, 1], zhi.at[sweep], w_ss.at[sweep, 1], w_rs.at[sweep, 1], (me, t_prev)),
+            copy(ubufs.at[sweep, top], zlo.at[sweep], w_ss.at[sweep, 0], w_rs.at[sweep, 0], (me, t_next)),
+            copy(ubufs.at[sweep, 0], zhi.at[sweep], w_ss.at[sweep, 1], w_rs.at[sweep, 1], (me, t_prev)),
             copy(xup.at[sweep], xlo.at[sweep], w_ss.at[sweep, 2], w_rs.at[sweep, 2], (s_next, t)),
             copy(xdn.at[sweep], xhi.at[sweep], w_ss.at[sweep, 3], w_rs.at[sweep, 3], (s_prev, t)),
         ]
-        for c in edge_copies:
-            c.start()
+        edge_copies[0].start()
+        edge_copies[1].start()
         sends += edge_copies
         flipped = ubuf[...].reshape(CELLS_HI, COLS).T
         weights = jnp.concatenate(split(flipped, 2), 0)
@@ -451,18 +453,27 @@
 
         def u_copy(d, sweep=sweep):
             return copy(
-                uown.at[sweep, d], urecv.at[sweep, others - 1 - d],
-                u_ss.at[sweep, d], u_rs.at[sweep, others - 1 - d], (sector_of(d + 1), t),
+                uown.at[sweep, d], urecv.at[sweep, mirror[d]],
+                u_ss.at[sweep, d], u_rs.at[sweep, mirror[d]], (sector_of(d), t),
             )
 
         weights = fsplit[0, :256]
-        for d in far_first:
-
-            def store(i, b, row, d=d):
-                uown[sweep, d, b : b + 1, :] = row
-
-            gather(d, [weights], 2, store)
-            u_copy(d).start()
+        for group in groups:
+            for d in group:
+
+                def store(i, b, row, d=d):
+                    uown[sweep, d, b : b + 1, :] = row
+
+                gather(d, [weights], 2, store)
+            if group is groups[1]:
+                for k in range(LAYERS):
+                    xup[sweep, k : k + 1, :] = ubuf[k, last:]
+                    xdn[sweep, k : k + 1, :] = ubuf[k, :1]
+            for d in group:
+                u_copy(d).start()
+            if group is groups[1]:
+                edge_copies[2].start()
+                edge_copies[3].start()
 
         for k in range(LAYERS):
             u = ubuf[k]
@@ -475,11 +486,17 @@
                 total = total + cz[k + 1] * ubuf[k + 1]
             part[k] = total
 
-        def arrived(d, sweep=sweep, u_copy=u_copy):
-            u_copy(others - 1 - d).wait_recv()
-            return urecv[sweep, d]
-
-        extra = fault_extra(arrivals, arrived)
+        total = None
+        for group in (groups[0] + groups[1], groups[2]):
+            for i in group:
+                u_copy(i).wait_recv()
+            for d in [mirror[i] for i in group]:
+                vals[d, 0] = link[d] * urecv[sweep, d]
+                placed = lax.dot_general(
+                    oh[d], masked(d, vals.at[d, 0]), nt, preferred_element_type=F32
+                )
+                total = placed if total is None else total + placed
+        extra = (total[:, :128] + total[:, 128:]).reshape(block_shape)
         for c in edge_copies:
             c.wait_recv()
         part[0] += cz[0] * zlo[sweep]
@@ -487,19 +504,19 @@
         for k in range(LAYERS):
             part[k, last:] += cxu[k, last:] * xhi[sweep, k : k + 1, :]
             part[k, :1] += cxd[k, :1] * xlo[sweep, k : k + 1, :]
-        target = out_ref if sweep == SWEEPS - 2 else ubuf
+        target = out_ref if sweep == SWEEPS - 2 else ubufs.at[sweep + 1]
         for k in range(LAYERS):
             target[k] = (1.0 - RELAXATION) * ubuf[k] + inv[k] * (part[k] + extra[k])
 
-    for c in halo_copies + sends:
+    for c in halo_copies + [up_copy] + sends:
         c.wait_send()
     for d in range(others):
         fault_copy(d).wait_send()
         a_copy(d).wait_send()
         for sweep in range(SWEEPS - 1):
             copy(
-                uown.at[sweep, d], urecv.at[sweep, others - 1 - d],
-                u_ss.at[sweep, d], u_rs.at[sweep, others - 1 - d], (sector_of(d + 1), t),
+                uown.at[sweep, d], urecv.at[sweep, mirror[d]],
+                u_ss.at[sweep, d], u_rs.at[sweep, mirror[d]], (sector_of(d), t),
             ).wait_send()
 
     @pl.loop(1, n_slab)
@@ -545,9 +562,9 @@
         far=f32(others, 4, *tiles),
         link=f32(others, *tiles),
         vals=f32(others, 4, *tiles),
-        up_stage=f32(5, ROWS, COLS),
+        up_stage=f32(4, ROWS, COLS),
         dn_stage=f32(3, ROWS, COLS),
-        halo_lo=f32(5, ROWS, COLS),
+        halo_lo=f32(4, ROWS, COLS),
         halo_hi=f32(3, ROWS, COLS),
         rup_stage=f32(5, LAYERS, COLS),
         rdn_stage=f32(3, LAYERS, COLS),
@@ -565,11 +582,11 @@
         storage=f32(*block),
         rhs=f32(*block),
         inv=f32(*block),
-        ubuf=f32(*block),
+        ubufs=f32(rounds, *block),
         part=f32(*block),
+        to_layer=f32(LAYERS, *block),
         uown=f32(rounds, others, *tiles),
         urecv=f32(rounds, others, *tiles),
-        usend=f32(rounds, 2, ROWS, COLS),
         zlo=f32(rounds, ROWS, COLS),
         zhi=f32(rounds, ROWS, COLS),
         xup=f32(rounds, LAYERS, COLS),

time: 57.2 us -> 59.5 us (1.040)
  Pallas kernels: 53.9 us -> 56.3 us
    pallas_call x1, Pallas kernels: 53.9 us -> 56.3 us  [body(): pl.pallas_call(run, out_shape=(jax.ShapeDtypeStruct((3, *block), F32), ja...]
where the time goes in v3:
time: 59.5 us; the launch traced here: 59.4 us
  Pallas kernels  56.3 us (95%)
  local copies, waits for them, and re-layouts  2.46 us (4%)
  between operations  0.65 us (1%)
    pallas_call x1, Pallas kernels, body(): pl.pallas_call(run, out_shape=(jax.ShapeDtypeStruct((3, *block), F32), ja...  56.3 us
    unnamed x4, local copies, waits for them, and re-layouts  2.46 us

profile of v3, /device:TPU:1, one launch (start us, length us, event | category | flops | bytes accessed | tf_op | source)
XLA Modules:
  0.0 59.4 jit_solution(8534045754175548661)
XLA Ops:
  0.6 56.3 %shard_map.113 = (f32[3,4,64,128]{3,2,1,0:T(8,128)}, f32[4,64,128]{2,1,0:T(8,128)}) custom-call(f32[4,64,128]{2,1,0:T(8,128)} %refs_0_.1, f32[2,4,64,128]{3,2,1,0:T(8,128)} %refs_1_.1, f32[3,4,64,128]{3,2,1,0:T(8,128)} %refs_2_.1, f32[4,64,128]{2,1,0:T(8,128)} %refs_3_.1, f32[3,4,64,128]{3,2,1,0:T(8,128)} %refs_4_.1, s32[4,64,128]{2,1,0:T(8,128)} %refs_5_.1, ...), custom_call_target="tpu_custom_call" | custom-call | tf_op jit(solution)/shard_map/pallas_call | solution.py:608
  56.9 0.0 copy-start
  56.9 1.8 %copy.14 = f32[3,4,64,128]{3,2,1,0:T(8,128)} copy(f32[3,4,64,128]{3,2,1,0:T(8,128)} %get-tuple-element.4) | data formatting | bytes 786432
  58.7 0.0 copy-done
  58.7 0.7 %copy.15 = f32[4,64,128]{2,1,0:T(8,128)} copy(f32[4,64,128]{2,1,0:T(8,128)S(1)} %copy-done) | data formatting | bytes 262144
Async XLA Ops:
  56.9 1.8 %copy-start = (f32[4,64,128]{2,1,0:T(8,128)S(1)}, f32[4,64,128]{2,1,0:T(8,128)}, u32[]{:S(2)}) copy-start(f32[4,64,128]{2,1,0:T(8,128)} %get-tuple-element.5) | copy-start | bytes 393220

commit v4 on v3

--- a/solution.py
+++ b/solution.py
@@ -55,7 +55,7 @@
     oh, ohlo, fsplit, cell, fweight, fup, own, far, link, vals,
     up_stage, dn_stage, halo_lo, halo_hi, rup_stage, rdn_stage, rhalo_lo, rhalo_hi,
     asend, arecv, bsend, brecv,
-    cz, cxu, cxd, cyu, cyd, storage, rhs, inv, ubufs, part, to_layer,
+    cz, cxu, cxd, cyu, cyd, storage, rhs, inv, ubufs, part,
     uown, urecv, zlo, zhi, xup, xdn, xlo, xhi,
     f_ss, f_rs, h_ss, h_rs, a_ss, a_rs, b_ss, b_rs, u_ss, u_rs, w_ss, w_rs,
 ):
@@ -79,9 +79,18 @@
     mirror = [partners.index(((chips - c) % chips, other)) for c, other in partners]
     chip, core = me // 2, lax.rem(me, 2)
 
+    sectors = [
+        lax.rem(chip + c, chips) * 2 + (1 - core if other else core) for c, other in partners
+    ]
+
     def sector_of(i):
-        c, other = partners[i]
-        return lax.rem(chip + c, chips) * 2 + (1 - core if other else core)
+        return sectors[i]
+
+    def take(ref, sem):
+        copy(ref, ref, sem, sem, (s_next, t)).wait_recv()
+
+    def sent(ref, sem):
+        copy(ref, ref, sem, sem, (s_next, t)).wait_send()
 
     held = (p_ref, s_ref, om_ref, pv_ref, tr_ref, bits_ref, fc_ref, cnt_ref, ft_ref, fu_ref)
     loads = [
@@ -167,7 +176,7 @@
                     store(i, 2 * b + k, jnp.sum(found, axis=0, keepdims=True))
 
     def fault_copy(d):
-        return copy(own.at[d], far.at[mirror[d]], f_ss.at[d], f_rs.at[mirror[d]],
+        return copy(own.at[d], far.at[mirror[d]], f_ss.at[0], f_rs.at[0],
                     (sector_of(d), t))
 
     for d in range(others):
@@ -235,8 +244,7 @@
 
     zero_tile = jnp.zeros((CHUNKS, 128), F32)
     layer_source = [zero_tile] * LAYERS
-    for d in range(others):
-        fault_copy(d).wait_recv()
+    take(far, f_rs.at[0])
     for d in range(others):
         flags = fup[d]
         w = fweight[d]
@@ -249,8 +257,9 @@
         vals[d, 3] = coupling
         link[d] = coupling
         layer = jnp.right_shift(cell[d], 13)
+        total = flux[0] + flux[1] + flux[2]
         for k in range(LAYERS):
-            layer_source[k] = layer_source[k] - jnp.where(layer == k, flux[2], 0.0)
+            layer_source[k] = layer_source[k] - jnp.where(layer == k, total, 0.0)
 
     nt = (((1,), (1,)), ((), ()))
 
@@ -273,10 +282,6 @@
             .T.reshape(LAYERS, ROWS, COLS)
             for i in range(len(fields))
         ]
-
-    placed = scatter((0, 1))
-    res_ref[0] += placed[0]
-    res_ref[1] += placed[1]
 
     for c in halo_copies:
         c.wait_recv()
@@ -335,20 +340,19 @@
         asend[8 + k : 9 + k, :] = source
 
     def a_copy(d):
-        return copy(asend, arecv.at[mirror[d]], a_ss.at[d], a_rs.at[mirror[d]],
+        return copy(asend, arecv.at[mirror[d]], a_ss.at[0], a_rs.at[0],
                     (sector_of(d), t))
 
     for d in range(others):
         a_copy(d).start()
     up_copy.start()
 
-    placed = scatter((2, 3))
-    res_ref[2] += placed[0]
-    inv[...] += placed[1]
+    placed = scatter((0, 1))
+    res_ref[0] += placed[0]
+    res_ref[1] += placed[1]
 
     sums = asend[...]
-    for d in range(others):
-        a_copy(d).wait_recv()
+    take(arecv, a_rs.at[0])
     for d in range(others):
         sums = sums + arecv[d]
     column = jnp.sum(sums, axis=1, keepdims=True)
@@ -363,7 +367,7 @@
     brecv[t] = bsend[...]
 
     def b_copy(k, dst):
-        return copy(bsend, brecv.at[dst], b_ss.at[k - 1], b_rs.at[k - 1],
+        return copy(bsend, brecv.at[dst], b_ss.at[0], b_rs.at[0],
                     (me, lax.rem(t + k, n_slab)))
 
     def hops(k):
@@ -373,14 +377,9 @@
     for k in sorted(range(1, n_slab), key=lambda k: (-hops(k), k)):
         b_copy(k, t).start()
 
-    for d in range(others):
-        for j in range(LAYERS):
-            vals[d, j] = jnp.where(far[d, 3] == j, link[d], 0.0)
-    for j in range(0, LAYERS, 2):
-        placed = scatter((j, j + 1))
-        to_layer[j] = placed[0]
-        to_layer[j + 1] = placed[1]
-
+    placed = scatter((2, 3))
+    res_ref[2] += placed[0]
+    inv[...] += placed[1]
     up_copy.wait_recv()
     cz[0] = halo_lo[3]
     inv[0] += halo_lo[3]
@@ -390,9 +389,7 @@
     for k in range(LAYERS):
         rhs[k] = -(res_ref[0, k] + res_ref[1, k] + res_ref[2, k])
 
-    @pl.loop(1, n_slab)
-    def _(k):
-        b_copy(k, lax.rem(t + n_slab - k, n_slab)).wait_recv()
+    take(brecv.at[pl.ds(0, n_slab - 1)], b_rs.at[0])
 
     lane4 = lax.broadcasted_iota(jnp.int32, (4, 128), 1)
     rows = jnp.zeros((4, 128), F32)
@@ -425,28 +422,43 @@
     def level_row(k):
         return level[k + 1 : k + 2]
 
+    def place(partners_now, values, total):
+        for d in partners_now:
+            vals[d, 0] = link[d] * values(d)
+            placed = lax.dot_general(
+                oh[d], masked(d, vals.at[d, 0]), nt, preferred_element_type=F32
+            )
+            total = placed if total is None else total + placed
+        return total
+
+    def extra_of(total):
+        return (total[:, :128] + total[:, 128:]).reshape(LAYERS, ROWS, COLS)
+
+    def coarse_far(d):
+        value = zero_tile
+        for k in range(LAYERS):
+            value = jnp.where(far[d, 3] == k, level_row(k), value)
+        return value
+
+    part[...] = extra_of(place(range(others), coarse_far, None))
     for k in range(LAYERS):
         here = level_row(k)
-        total = rhs[k] + cz[k + 1] * level_row(k + 1) + cz[k] * level_row(k - 1)
+        total = part[k] + rhs[k] + cz[k + 1] * level_row(k + 1) + cz[k] * level_row(k - 1)
         total = total + (cxu[k] + cxd[k] + cyu[k] + cyd[k]) * here
-        for j in range(LAYERS):
-            total = total + to_layer[j, k] * level_row(j)
         ubufs[0, k] = (1.0 - RELAXATION) * here + inv[k] * total
 
-    block_shape = (LAYERS, ROWS, COLS)
     groups = [list(range(2)), list(range(2, 4)), list(range(4, others))]
-    sends = []
+    group_of = {d: g for g, group in enumerate(groups) for d in group}
     for sweep in range(SWEEPS - 1):
         ubuf = ubufs.at[sweep]
         edge_copies = [
-            copy(ubufs.at[sweep, top], zlo.at[sweep], w_ss.at[sweep, 0], w_rs.at[sweep, 0], (me, t_next)),
-            copy(ubufs.at[sweep, 0], zhi.at[sweep], w_ss.at[sweep, 1], w_rs.at[sweep, 1], (me, t_prev)),
-            copy(xup.at[sweep], xlo.at[sweep], w_ss.at[sweep, 2], w_rs.at[sweep, 2], (s_next, t)),
-            copy(xdn.at[sweep], xhi.at[sweep], w_ss.at[sweep, 3], w_rs.at[sweep, 3], (s_prev, t)),
+            copy(ubufs.at[sweep, top], zlo.at[sweep], w_ss.at[0], w_rs.at[sweep, 0], (me, t_next)),
+            copy(ubufs.at[sweep, 0], zhi.at[sweep], w_ss.at[0], w_rs.at[sweep, 1], (me, t_prev)),
+            copy(xup.at[sweep], xlo.at[sweep], w_ss.at[1], w_rs.at[sweep, 2], (s_next, t)),
+            copy(xdn.at[sweep], xhi.at[sweep], w_ss.at[2], w_rs.at[sweep, 3], (s_prev, t)),
         ]
         edge_copies[0].start()
         edge_copies[1].start()
-        sends += edge_copies
         flipped = ubuf[...].reshape(CELLS_HI, COLS).T
         weights = jnp.concatenate(split(flipped, 2), 0)
         fsplit[0, :256, :] = weights
@@ -454,7 +466,7 @@
         def u_copy(d, sweep=sweep):
             return copy(
                 uown.at[sweep, d], urecv.at[sweep, mirror[d]],
-                u_ss.at[sweep, d], u_rs.at[sweep, mirror[d]], (sector_of(d), t),
+                u_ss.at[0], u_rs.at[sweep, group_of[d]], (sector_of(d), t),
             )
 
         weights = fsplit[0, :256]
@@ -487,16 +499,10 @@
             part[k] = total
 
         total = None
-        for group in (groups[0] + groups[1], groups[2]):
-            for i in group:
-                u_copy(i).wait_recv()
-            for d in [mirror[i] for i in group]:
-                vals[d, 0] = link[d] * urecv[sweep, d]
-                placed = lax.dot_general(
-                    oh[d], masked(d, vals.at[d, 0]), nt, preferred_element_type=F32
-                )
-                total = placed if total is None else total + placed
-        extra = (total[:, :128] + total[:, 128:]).reshape(block_shape)
+        for g, group in enumerate(groups):
+            take(urecv.at[sweep, pl.ds(0, len(group))], u_rs.at[sweep, g])
+            total = place([mirror[i] for i in group], lambda d: urecv[sweep, d], total)
+        extra = extra_of(total)
         for c in edge_copies:
             c.wait_recv()
         part[0] += cz[0] * zlo[sweep]
@@ -508,20 +514,15 @@
         for k in range(LAYERS):
             target[k] = (1.0 - RELAXATION) * ubuf[k] + inv[k] * (part[k] + extra[k])
 
-    for c in halo_copies + [up_copy] + sends:
+    for c in halo_copies + [up_copy]:
         c.wait_send()
-    for d in range(others):
-        fault_copy(d).wait_send()
-        a_copy(d).wait_send()
-        for sweep in range(SWEEPS - 1):
-            copy(
-                uown.at[sweep, d], urecv.at[sweep, mirror[d]],
-                u_ss.at[sweep, d], u_rs.at[sweep, mirror[d]], (sector_of(d), t),
-            ).wait_send()
-
-    @pl.loop(1, n_slab)
-    def _(k):
-        b_copy(k, t).wait_send()
+    sent(far, f_ss.at[0])
+    sent(arecv, a_ss.at[0])
+    sent(brecv.at[pl.ds(0, n_slab - 1)], b_ss.at[0])
+    sent(urecv, u_ss.at[0])
+    sent(ubufs.at[:, pl.ds(0, 2)], w_ss.at[0])
+    sent(xup, w_ss.at[1])
+    sent(xdn, w_ss.at[2])
 
 
 def body(n_sector, n_slab, *args):
@@ -584,7 +585,6 @@
         inv=f32(*block),
         ubufs=f32(rounds, *block),
         part=f32(*block),
-        to_layer=f32(LAYERS, *block),
         uown=f32(rounds, others, *tiles),
         urecv=f32(rounds, others, *tiles),
         zlo=f32(rounds, ROWS, COLS),
@@ -593,12 +593,12 @@
         xdn=f32(rounds, LAYERS, COLS),
         xlo=f32(rounds, LAYERS, COLS),
         xhi=f32(rounds, LAYERS, COLS),
-        f_ss=sem(others), f_rs=sem(others),
+        f_ss=sem(1), f_rs=sem(1),
         h_ss=sem(4), h_rs=sem(4),
-        a_ss=sem(others), a_rs=sem(others),
-        b_ss=sem(n_slab - 1), b_rs=sem(n_slab - 1),
-        u_ss=sem(rounds, others), u_rs=sem(rounds, others),
-        w_ss=sem(rounds, 4), w_rs=sem(rounds, 4),
+        a_ss=sem(1), a_rs=sem(1),
+        b_ss=sem(1), b_rs=sem(1),
+        u_ss=sem(1), u_rs=sem(rounds, 3),
+        w_ss=sem(3), w_rs=sem(rounds, 4),
     )
     names = list(scratch)
 

time: 59.5 us -> 56.8 us (0.955)
  Pallas kernels: 56.3 us -> 53.6 us
    pallas_call x1, Pallas kernels: 56.3 us -> 53.6 us  [body(): pl.pallas_call(run, out_shape=(jax.ShapeDtypeStruct((3, *block), F32), ja...]
where the time goes in v4:
time: 56.8 us; the launch traced here: 56.7 us
  Pallas kernels  53.6 us (94%)
  local copies, waits for them, and re-layouts  2.46 us (4%)
  between operations  0.65 us (1%)
    pallas_call x1, Pallas kernels, body(): pl.pallas_call(run, out_shape=(jax.ShapeDtypeStruct((3, *block), F32), ja...  53.6 us
    unnamed x4, local copies, waits for them, and re-layouts  2.46 us

profile of v4, /device:TPU:1, one launch (start us, length us, event | category | flops | bytes accessed | tf_op | source)
XLA Modules:
  0.0 56.7 jit_solution(13657649697291168991)
XLA Ops:
  0.6 53.6 %shard_map.113 = (f32[3,4,64,128]{3,2,1,0:T(8,128)}, f32[4,64,128]{2,1,0:T(8,128)}) custom-call(f32[4,64,128]{2,1,0:T(8,128)} %refs_0_.1, f32[2,4,64,128]{3,2,1,0:T(8,128)} %refs_1_.1, f32[3,4,64,128]{3,2,1,0:T(8,128)} %refs_2_.1, f32[4,64,128]{2,1,0:T(8,128)} %refs_3_.1, f32[3,4,64,128]{3,2,1,0:T(8,128)} %refs_4_.1, s32[4,64,128]{2,1,0:T(8,128)} %refs_5_.1, ...), custom_call_target="tpu_custom_call" | custom-call | tf_op jit(solution)/shard_map/pallas_call | solution.py:608
  54.2 0.0 copy-start
  54.3 1.8 %copy.14 = f32[3,4,64,128]{3,2,1,0:T(8,128)} copy(f32[3,4,64,128]{3,2,1,0:T(8,128)} %get-tuple-element.4) | data formatting | bytes 786432
  56.1 0.0 copy-done
  56.1 0.7 %copy.15 = f32[4,64,128]{2,1,0:T(8,128)} copy(f32[4,64,128]{2,1,0:T(8,128)S(1)} %copy-done) | data formatting | bytes 262144
Async XLA Ops:
  54.2 1.8 %copy-start = (f32[4,64,128]{2,1,0:T(8,128)S(1)}, f32[4,64,128]{2,1,0:T(8,128)}, u32[]{:S(2)}) copy-start(f32[4,64,128]{2,1,0:T(8,128)} %get-tuple-element.5) | copy-start | bytes 393220

commit v5 on v4

--- a/solution.py
+++ b/solution.py
@@ -457,8 +457,6 @@
             copy(xup.at[sweep], xlo.at[sweep], w_ss.at[1], w_rs.at[sweep, 2], (s_next, t)),
             copy(xdn.at[sweep], xhi.at[sweep], w_ss.at[2], w_rs.at[sweep, 3], (s_prev, t)),
         ]
-        edge_copies[0].start()
-        edge_copies[1].start()
         flipped = ubuf[...].reshape(CELLS_HI, COLS).T
         weights = jnp.concatenate(split(flipped, 2), 0)
         fsplit[0, :256, :] = weights
@@ -483,6 +481,9 @@
                     xdn[sweep, k : k + 1, :] = ubuf[k, :1]
             for d in group:
                 u_copy(d).start()
+            if group is groups[0]:
+                edge_copies[0].start()
+                edge_copies[1].start()
             if group is groups[1]:
                 edge_copies[2].start()
                 edge_copies[3].start()

time: 56.8 us -> 56.8 us (level)
  no operation moved by 1% of the time
where the time goes in v5:
time: 56.8 us; the launch traced here: 56.6 us
  Pallas kernels  53.5 us (94%)
  local copies, waits for them, and re-layouts  2.46 us (4%)
  between operations  0.65 us (1%)
    pallas_call x1, Pallas kernels, body(): pl.pallas_call(run, out_shape=(jax.ShapeDtypeStruct((3, *block), F32), ja...  53.5 us
    unnamed x4, local copies, waits for them, and re-layouts  2.46 us

profile of v5, /device:TPU:1, one launch (start us, length us, event | category | flops | bytes accessed | tf_op | source)
XLA Modules:
  0.0 56.6 jit_solution(5160187221032944632)
XLA Ops:
  0.6 53.5 %shard_map.113 = (f32[3,4,64,128]{3,2,1,0:T(8,128)}, f32[4,64,128]{2,1,0:T(8,128)}) custom-call(f32[4,64,128]{2,1,0:T(8,128)} %refs_0_.1, f32[2,4,64,128]{3,2,1,0:T(8,128)} %refs_1_.1, f32[3,4,64,128]{3,2,1,0:T(8,128)} %refs_2_.1, f32[4,64,128]{2,1,0:T(8,128)} %refs_3_.1, f32[3,4,64,128]{3,2,1,0:T(8,128)} %refs_4_.1, s32[4,64,128]{2,1,0:T(8,128)} %refs_5_.1, ...), custom_call_target="tpu_custom_call" | custom-call | tf_op jit(solution)/shard_map/pallas_call | solution.py:609
  54.2 0.0 copy-start
  54.2 1.8 %copy.14 = f32[3,4,64,128]{3,2,1,0:T(8,128)} copy(f32[3,4,64,128]{3,2,1,0:T(8,128)} %get-tuple-element.4) | data formatting | bytes 786432
  56.0 0.0 copy-done
  56.0 0.7 %copy.15 = f32[4,64,128]{2,1,0:T(8,128)} copy(f32[4,64,128]{2,1,0:T(8,128)S(1)} %copy-done) | data formatting | bytes 262144
Async XLA Ops:
  54.2 1.8 %copy-start = (f32[4,64,128]{2,1,0:T(8,128)S(1)}, f32[4,64,128]{2,1,0:T(8,128)}, u32[]{:S(2)}) copy-start(f32[4,64,128]{2,1,0:T(8,128)} %get-tuple-element.5) | copy-start | bytes 393220
